TPU v7x, 512 devices: a whole 4x4x16 slice. The times are simulated.
512 devices in a mesh: tm: 32 (over z_lo, y, core), rows: 16 (over z_hi, x).
Axes of the slice: x: 4, y: 4, z: 16 (z_hi: 4, z_lo: 4; z = z_hi * 4 + z_lo), core: 2. Of those that a mesh axis runs over, the one named last changes fastest.
Arguments:
- video: bfloat16 [64, 64, 120, 128], P('tm', 'rows'), may hold values from -6 to 6
- norm_gain: bfloat16 [128], replicated, may hold values from 0.099609375 to 1.8984375
- conv_first: bfloat16 [3, 3, 3, 128, 128], replicated, may hold values from -0.109375 to 0.109375
- conv_second: bfloat16 [3, 3, 3, 128, 128], replicated, may hold values from -0.109375 to 0.109375
- attn_gain: bfloat16 [128], replicated, may hold values from 0.099609375 to 1.8984375
- query_weight: bfloat16 [128, 128], replicated, may hold values from -2 to 2
- key_weight: bfloat16 [128, 128], replicated, may hold values from -2 to 2
- value_weight: bfloat16 [128, 128], replicated, may hold values from -0.5 to 0.5
- out_weight: bfloat16 [128, 128], replicated, may hold values from -0.5 to 0.5
Outputs:
- result: bfloat16 [64, 64, 120, 128], P('tm', 'rows')
All inputs are finite; a program needn't handle non-finite values.
Results may differ from a plain program's by a relative error of at most 0.013.
Values may be sent and summed in bfloat16 or wider, within the bound.
A program may use at most 64 MiB of HBM per device.

v0:
```python
import jax
import jax.numpy as jnp
from jax import lax
from jax.sharding import PartitionSpec as P


def shifted(value, axis, steps):
    count = lax.axis_size(axis)
    leading, last = (max(0, -steps), min(count, count - steps))
    return lax.ppermute(value, axis, [(source, source + steps) for source in range(leading, last)])


def with_halo(x, sides, width):
    for axis, dim in sides:
        size, length = (lax.axis_size(axis), x.shape[dim])
        up = [(i, (i + 1) % size) for i in range(size - 1)]
        down = [(j, i) for i, j in up]
        last = lax.slice_in_dim(x, length - width, length, axis=dim)
        leading = lax.slice_in_dim(x, 0, width, axis=dim)
        before = lax.ppermute(last, axis, up)
        after = lax.ppermute(leading, axis, down)
        x = jnp.concatenate([before, x, after], axis=dim)
    return x


def rms_norm(values, gain):
    wide = values.astype(jnp.float32)
    scale = lax.rsqrt(jnp.mean(wide * wide, axis=-1, keepdims=True) + 1e-06)
    return wide * scale * gain.astype(jnp.float32)


def convolve(field, kernel):
    frames, height, width, chans = field.shape
    earlier = shifted(field, "tm", 1)
    extended = jnp.concatenate([earlier, field], axis=0)
    padded = with_halo(extended, (("rows", 1),), 1)
    padded = jnp.pad(padded, ((0, 0), (0, 0), (1, 1), (0, 0)))
    total = jnp.zeros((frames * height * width, chans), jnp.float32)
    for shift_t in range(3):
        for shift_h in range(3):
            slab = padded[shift_t : shift_t + frames, shift_h : shift_h + height]
            joined = jnp.concatenate([slab[:, :, e : e + width] for e in range(3)], axis=-1)
            taps = kernel[shift_t, shift_h].reshape(3 * chans, chans)
            total = total + jnp.dot(
                joined.reshape(-1, 3 * chans), taps, preferred_element_type=jnp.float32
            )
    return total.reshape(frames, height, width, chans)


def block_scores(query, keys, query_first):
    chans = query.shape[-1]
    scores = jnp.einsum("fpc,gpc->fgp", query, keys, preferred_element_type=jnp.float32) / jnp.sqrt(
        jnp.float32(chans)
    )
    query_pos = query_first + jnp.arange(query.shape[0], dtype=jnp.int32)
    key_pos = jnp.arange(keys.shape[0], dtype=jnp.int32)
    allowed = (key_pos[None, :] <= query_pos[:, None])[:, :, None]
    tile_top = jnp.max(jnp.where(allowed, scores, jnp.float32(-1e30)), axis=1)
    return (scores, allowed, tile_top)


def absorb_block(carry, query, keys, values, query_first):
    top, total, acc = carry
    scores, allowed, tile_top = block_scores(query, keys, query_first)
    new_top = jnp.maximum(top, tile_top)
    weights = jnp.where(allowed, jnp.exp(scores - new_top[:, None, :]), jnp.float32(0.0))
    total = jnp.sum(weights, axis=1)
    update = jnp.einsum(
        "fgp,gpc->fpc", weights.astype(jnp.bfloat16), values, preferred_element_type=jnp.float32
    )
    acc = update
    return (new_top, total, acc)


def start_carry(frames, cells, chans):
    return (
        jnp.full((frames, cells), -1e30, jnp.float32),
        jnp.zeros((frames, cells), jnp.float32),
        jnp.zeros((frames, cells, chans), jnp.float32),
    )


def local(
    video,
    norm_gain,
    conv_first,
    conv_second,
    attn_gain,
    query_weight,
    key_weight,
    value_weight,
    out_weight,
):
    frames, height, width, chans = video.shape
    act = jax.nn.silu(rms_norm(video, norm_gain)).astype(jnp.bfloat16)
    mid = jax.nn.silu(convolve(act, conv_first)).astype(jnp.bfloat16)
    hidden = (video.astype(jnp.float32) + convolve(mid, conv_second)).astype(jnp.bfloat16)
    normed = rms_norm(hidden, attn_gain).astype(jnp.bfloat16)
    flat = normed.reshape(-1, chans)
    joined_weight = jnp.concatenate([query_weight, key_weight, value_weight], axis=1)
    projected = jnp.dot(flat, joined_weight, preferred_element_type=jnp.float32).astype(
        jnp.bfloat16
    )
    cells = height * width
    query = projected[:, :chans].reshape(frames, cells, chans)
    keys = projected[:, chans : 2 * chans].reshape(frames, cells, chans)
    values = projected[:, 2 * chans :].reshape(frames, cells, chans)
    query_first = lax.axis_index("tm") * frames
    top, total, acc = absorb_block(
        start_carry(frames, cells, chans),
        query,
        lax.all_gather(keys, "tm", axis=0, tiled=True),
        lax.all_gather(values, "tm", axis=0, tiled=True),
        query_first,
    )
    mixed = (acc / total[:, :, None]).astype(jnp.bfloat16)
    output = jnp.dot(mixed.reshape(-1, chans), out_weight, preferred_element_type=jnp.float32)
    result = hidden.reshape(-1, chans).astype(jnp.float32) + output
    return result.astype(jnp.bfloat16).reshape(frames, height, width, chans)


def solution(mesh):
    return jax.shard_map(
        local,
        mesh=mesh,
        in_specs=(P("tm", "rows", None, None), P(), P(), P(), P(), P(), P(), P(), P()),
        out_specs=P("tm", "rows", None, None),
        check_vma=False,
    )
```

profile of v0, /device:TPU:1, one launch (start us, length us, event | category | flops | bytes accessed | tf_op | source)
XLA Modules:
  0.0 247.9 jit_solution(13265334246154741844)
XLA Ops:
  6.5 1.2 fusion.26
  7.8 0.7 convert_element_type.47
  8.5 1.2 fusion.33
  9.6 4.6 %collective-permute-start = (bf16[2,4,120,128]{3,2,1,0:T(8,128)(2,1)S(1)}, bf16[2,4,120,128]{3,2,1,0:T(8,128)(2,1)S(1)}, u32[]{:S(2)}, u32[]{:S(2)}) collective-permute-start(bf16[2,4,120,128]{3,2,1,0:T(8,128)(2,1)S(1)} %fusion.33), channel_id=1, source_target_pairs={{0,16},{16,32},{32,48},{48,64},{64,80},{80,96},{96,112},{112,128},... | collective-permute-start | bytes 737288 | tf_op jit(solution)/shard_map/ppermute | solution.py:10
  14.2 4.6 %collective-permute-done = bf16[2,4,120,128]{3,2,1,0:T(8,128)(2,1)S(1)} collective-permute-done((bf16[2,4,120,128]{3,2,1,0:T(8,128)(2,1)S(1)}, bf16[2,4,120,128]{3,2,1,0:T(8,128)(2,1)S(1)}, u32[]{:S(2)}, u32[]{:S(2)}) %collective-permute-start) | collective-permute-done | bytes 245792 | tf_op jit(solution)/shard_map/ppermute | solution.py:10
  18.8 1.7 collective-permute-start.1
  20.5 1.3 collective-permute-start.2
  21.9 1.7 collective-permute-done.1
  23.6 3.9 %collective-permute-done.2 = bf16[4,1,120,128]{3,2,1,0:T(8,128)(2,1)S(1)} collective-permute-done((bf16[4,1,120,128]{3,2,1,0:T(8,128)(2,1)S(1)}, bf16[4,1,120,128]{3,2,1,0:T(8,128)(2,1)S(1)}, u32[]{:S(2)}, u32[]{:S(2)}) %collective-permute-start.2) | collective-permute-done | bytes 122912 | tf_op jit(solution)/shard_map/ppermute | solution.py:21
  27.5 0.3 fusion.19
  27.8 0.6 fusion.51
  28.9 0.3 fusion.57
  29.3 0.4 pad_maximum_fusion.8
  29.7 0.4 convolution_add_fusion.16
  30.0 0.4 convolution_add_fusion.15
  30.6 0.4 convolution_add_fusion.14
  31.0 0.4 convolution_add_fusion.13
  31.3 0.4 convolution_add_fusion.12
  31.7 0.4 convolution_add_fusion.11
  32.1 0.4 convolution_add_fusion.10
  32.5 0.4 convolution_add_fusion.9
  33.1 4.4 %collective-permute-start.3 = (bf16[2,4,120,128]{3,2,1,0:T(8,128)(2,1)S(1)}, bf16[2,4,120,128]{3,2,1,0:T(8,128)(2,1)S(1)}, u32[]{:S(2)}, u32[]{:S(2)}) collective-permute-start(bf16[2,4,120,128]{3,2,1,0:T(8,128)(2,1)S(1)} %multiply_convert_fusion.1), channel_id=1, source_target_pairs={{0,16},{16,32},{32,48},{48,64},{64,80},{80,96},{96,112},{112,128},... | collective-permute-start | bytes 737288 | tf_op jit(solution)/shard_map/ppermute | solution.py:10
  37.5 3.1 %collective-permute-done.3 = bf16[2,4,120,128]{3,2,1,0:T(8,128)(2,1)S(1)} collective-permute-done((bf16[2,4,120,128]{3,2,1,0:T(8,128)(2,1)S(1)}, bf16[2,4,120,128]{3,2,1,0:T(8,128)(2,1)S(1)}, u32[]{:S(2)}, u32[]{:S(2)}) %collective-permute-start.3) | collective-permute-done | bytes 245792 | tf_op jit(solution)/shard_map/ppermute | solution.py:10
  40.6 3.1 %collective-permute-start.4 = (bf16[4,1,120,128]{3,2,1,0:T(8,128)(2,1)S(1)}, bf16[4,1,120,128]{3,2,1,0:T(8,128)(2,1)S(1)}, u32[]{:S(2)}, u32[]{:S(2)}) collective-permute-start(bf16[4,1,120,128]{3,2,1,0:T(8,128)(2,1)S(1)} %get-tuple-element.78), channel_id=1, source_target_pairs={{0,1},{1,2},{2,3},{3,4},{4,5},{5,6},{6,7},{7,8},{8,9},{9,10},{10,1... | collective-permute-start | bytes 368648 | tf_op jit(solution)/shard_map/ppermute | solution.py:20
  43.8 1.3 collective-permute-start.5
  45.2 0.4 collective-permute-done.4
  45.6 8.3 %collective-permute-done.5 = bf16[4,1,120,128]{3,2,1,0:T(8,128)(2,1)S(1)} collective-permute-done((bf16[4,1,120,128]{3,2,1,0:T(8,128)(2,1)S(1)}, bf16[4,1,120,128]{3,2,1,0:T(8,128)(2,1)S(1)}, u32[]{:S(2)}, u32[]{:S(2)}) %collective-permute-start.5) | collective-permute-done | bytes 122912 | tf_op jit(solution)/shard_map/ppermute | solution.py:21
  54.2 0.3 select_maximum_fusion
  54.5 0.6 fusion.50
  55.3 0.4 fusion.58
  56.2 0.3 pad_maximum_fusion.16
  56.5 0.4 convolution_add_fusion.8
  56.8 0.4 convolution_add_fusion.7
  57.2 0.4 convolution_add_fusion.6
  57.5 0.4 convolution_add_fusion.5
  57.9 0.4 convolution_add_fusion.4
  58.3 0.4 convolution_add_fusion.3
  58.6 0.4 convolution_add_fusion.2
  59.0 0.4 convolution_add_fusion.1
  60.0 0.3 convolution_convert_fusion
  60.4 0.9 fusion.52
  61.6 0.5 all-gather.3.cloned.1.call-update
  62.2 96.7 %all-gather.5.cloned.1.call-done = bf16[64,480,128]{2,1,0:T(8,128)(2,1)} async-done(((bf16[2,480,128]{2,1,0:T(8,128)(2,1)}), bf16[64,480,128]{2,1,0:T(8,128)(2,1)}) %all-gather.5.cloned.1.call-update) | async-done | bytes 7864336 | tf_op jit(solution)/shard_map/all_gather | solution.py:112
  158.9 7.5 %select_reduce_fusion = (f32[2,480]{0,1:T(8,128)S(1)}, f32[2,64,480]{1,0,2:T(2,128)S(1)}) fusion(pred[2,64]{1,0:T(4,128)(4,1)S(1)} %iota_compare_fusion.2, bf16[2,480,128]{2,1,0:T(8,128)(2,1)S(1)} %bitcast.133, bf16[64,480,128]{2,1,0:T(8,128)(2,1)} %all-gather.5.cloned.1.call-done), kind=kOutput, calls=%fused_computation.81 | convolution fusion | flops 15912000 | bytes 8359808 | tf_op jit(solution)/shard_map/fpc,gpc->fgp/dot_general | solution.py:52
  166.5 1.5 fusion.44
  168.1 65.8 %all-gather.3.cloned.1.call-done = bf16[64,480,128]{2,1,0:T(8,128)(2,1)} async-done(((bf16[2,480,128]{2,1,0:T(8,128)(2,1)}), bf16[64,480,128]{2,1,0:T(8,128)(2,1)}) %all-gather.3.cloned.1.call-update) | async-done | bytes 7864336 | tf_op jit(solution)/shard_map/all_gather | solution.py:113
  233.9 6.1 %fusion = f32[480,128,2]{1,2,0:T(2,128)S(1)} fusion(bf16[64,480,128]{2,1,0:T(8,128)(2,1)} %all-gather.3.cloned.1.call-done, f32[2,64,480]{1,0,2:T(2,128)S(1)} %get-tuple-element.91, pred[2,64]{1,0:T(4,128)(4,1)S(1)} %iota_compare_fusion.2, f32[2,480]{0,1:T(8,128)S(1)} %broadcast_maximum_fusion), kind=kOutput, calls=%fused_computation | convolution fusion | flops 15912960 | bytes 8605568 | tf_op jit(solution)/shard_map/fgp,gpc->fpc/dot_general | solution.py:68
  240.2 0.9 fusion.5
  (49 shorter events, 3.4 us)
Async XLA Ops:
  6.5 233.6 %copy-start = (bf16[128,128]{1,0:T(8,128)(2,1)S(1)}, bf16[128,128]{1,0:T(8,128)(2,1)}, u32[]{:S(2)}) copy-start(bf16[128,128]{1,0:T(8,128)(2,1)} %param.17) | copy-start | bytes 98308
  6.5 15.3 %copy-start.2 = (bf16[3,3,3,128,128]{4,3,2,1,0:T(8,128)(2,1)S(1)}, bf16[3,3,3,128,128]{4,3,2,1,0:T(8,128)(2,1)}, u32[]{:S(2)}) copy-start(bf16[3,3,3,128,128]{4,3,2,1,0:T(8,128)(2,1)} %param.11) | copy-start | bytes 2654212
  6.5 152.4 %all-gather.5.cloned.1.call-start = ((), (), s32[]{:S(2)}) async-start(), calls=%async_computation.1 | async-start | bytes 8110080 | tf_op jit(solution)/shard_map/all_gather | solution.py:112
  9.6 9.2 %collective-permute-start = (bf16[2,4,120,128]{3,2,1,0:T(8,128)(2,1)S(1)}, bf16[2,4,120,128]{3,2,1,0:T(8,128)(2,1)S(1)}, u32[]{:S(2)}, u32[]{:S(2)}) collective-permute-start(bf16[2,4,120,128]{3,2,1,0:T(8,128)(2,1)S(1)} %fusion.33), channel_id=1, source_target_pairs={{0,16},{16,32},{32,48},{48,64},{64,80},{80,96},{96,112},{112,128},... | collective-permute-start | bytes 737288 | tf_op jit(solution)/shard_map/ppermute | solution.py:10
  18.8 4.8 %collective-permute-start.1 = (bf16[4,1,120,128]{3,2,1,0:T(8,128)(2,1)S(1)}, bf16[4,1,120,128]{3,2,1,0:T(8,128)(2,1)S(1)}, u32[]{:S(2)}, u32[]{:S(2)}) collective-permute-start(bf16[4,1,120,128]{3,2,1,0:T(8,128)(2,1)S(1)} %get-tuple-element.82), channel_id=1, source_target_pairs={{0,1},{1,2},{2,3},{3,4},{4,5},{5,6},{6,7},{7,8},{8,9},{9,10},{10,1... | collective-permute-start | bytes 368648 | tf_op jit(solution)/shard_map/ppermute | solution.py:20
  20.5 7.0 %collective-permute-start.2 = (bf16[4,1,120,128]{3,2,1,0:T(8,128)(2,1)S(1)}, bf16[4,1,120,128]{3,2,1,0:T(8,128)(2,1)S(1)}, u32[]{:S(2)}, u32[]{:S(2)}) collective-permute-start(bf16[4,1,120,128]{3,2,1,0:T(8,128)(2,1)S(1)} %get-tuple-element.83), channel_id=1, source_target_pairs={{1,0},{2,1},{3,2},{4,3},{5,4},{6,5},{7,6},{8,7},{9,8},{10,9},{11,1... | collective-permute-start | bytes 368648 | tf_op jit(solution)/shard_map/ppermute | solution.py:21
  32.5 12.5 %copy-start.3 = (bf16[3,3,3,128,128]{4,3,2,1,0:T(8,128)(2,1)S(1)}, bf16[3,3,3,128,128]{4,3,2,1,0:T(8,128)(2,1)}, u32[]{:S(2)}) copy-start(bf16[3,3,3,128,128]{4,3,2,1,0:T(8,128)(2,1)} %param.12) | copy-start | bytes 2654212
  32.9 12.3 %copy-start.7 = (bf16[128]{0:T(256)(128)(2,1)S(1)}, bf16[128]{0:T(256)(128)(2,1)}, u32[]{:S(2)}) copy-start(bf16[128]{0:T(256)(128)(2,1)} %param.13) | copy-start | bytes 772
  33.1 7.5 %collective-permute-start.3 = (bf16[2,4,120,128]{3,2,1,0:T(8,128)(2,1)S(1)}, bf16[2,4,120,128]{3,2,1,0:T(8,128)(2,1)S(1)}, u32[]{:S(2)}, u32[]{:S(2)}) collective-permute-start(bf16[2,4,120,128]{3,2,1,0:T(8,128)(2,1)S(1)} %multiply_convert_fusion.1), channel_id=1, source_target_pairs={{0,16},{16,32},{32,48},{48,64},{64,80},{80,96},{96,112},{112,128},... | collective-permute-start | bytes 737288 | tf_op jit(solution)/shard_map/ppermute | solution.py:10
  40.6 5.0 %collective-permute-start.4 = (bf16[4,1,120,128]{3,2,1,0:T(8,128)(2,1)S(1)}, bf16[4,1,120,128]{3,2,1,0:T(8,128)(2,1)S(1)}, u32[]{:S(2)}, u32[]{:S(2)}) collective-permute-start(bf16[4,1,120,128]{3,2,1,0:T(8,128)(2,1)S(1)} %get-tuple-element.78), channel_id=1, source_target_pairs={{0,1},{1,2},{2,3},{3,4},{4,5},{5,6},{6,7},{7,8},{8,9},{9,10},{10,1... | collective-permute-start | bytes 368648 | tf_op jit(solution)/shard_map/ppermute | solution.py:20
  43.8 10.2 %collective-permute-start.5 = (bf16[4,1,120,128]{3,2,1,0:T(8,128)(2,1)S(1)}, bf16[4,1,120,128]{3,2,1,0:T(8,128)(2,1)S(1)}, u32[]{:S(2)}, u32[]{:S(2)}) collective-permute-start(bf16[4,1,120,128]{3,2,1,0:T(8,128)(2,1)S(1)} %get-tuple-element.79), channel_id=1, source_target_pairs={{1,0},{2,1},{3,2},{4,3},{5,4},{6,5},{7,6},{8,7},{9,8},{10,9},{11,1... | collective-permute-start | bytes 368648 | tf_op jit(solution)/shard_map/ppermute | solution.py:21
  58.6 0.9 copy-start.1
  59.0 1.0 copy-start.4
  59.0 1.0 copy-start.5
  59.0 1.0 copy-start.6
  61.3 172.5 %all-gather.3.cloned.1.call-start = ((), (), s32[]{:S(2)}) async-start(), calls=%async_computation | async-start | bytes 8110080 | tf_op jit(solution)/shard_map/all_gather | solution.py:113
Sparse Core Ops, SparseCore 0:
  61.4 97.4 all-gather.4
  161.1 72.7 all-gather.2
where the time goes:
time: 248 us
  waiting for transfers between devices  185 us (75%)
  matrix products  21.2 us (9%)
  starting transfers between devices  16.6 us (7%)
  between operations  14 us (6%)
  other arithmetic  8.13 us (3%)
  local copies, waits for them, and re-layouts  2.88 us (1%)
    all_gather x1, waiting for transfers between devices, local(): lax.all_gather(keys, 'tm', axis=0, tiled=True)  96.7 us
    all_gather x1, waiting for transfers between devices, local(): lax.all_gather(values, 'tm', axis=0, tiled=True)  65.8 us
    ppermute x2, waiting for transfers between devices, with_halo(): after = lax.ppermute(leading, axis, down)  12.2 us
    ppermute x2, starting transfers between devices, shifted(): lax.ppermute(value, axis, [(source, source + steps) for source in range(l...  9.02 us
    ppermute x2, waiting for transfers between devices, shifted(): lax.ppermute(value, axis, [(source, source + steps) for source in range(l...  7.68 us
    dot_general x1, matrix products, block_scores(): jnp.einsum('fpc,gpc->fgp', query, keys, preferred_element_type=jnp.float32)  7.5 us
    dot_general x18, matrix products, convolve(): jnp.dot(joined.reshape(-1, 3 * chans), taps, preferred_element_type=jnp.f...  6.36 us
    dot_general x1, matrix products, absorb_block(): jnp.einsum('fgp,gpc->fpc', weights.astype(jnp.bfloat16), values, preferre...  6.08 us
  transfers between devices with their start and end apart: 8, of which 8 were waited for; matrix products, arithmetic and copies ran while one was open for 4% of the time, Pallas kernels for 0%

commit v1 on v0

v1 whole, which is shorter than its diff:
```python
import functools

import jax
import jax.numpy as jnp
from jax import lax
from jax.experimental import pallas as pl
from jax.experimental.pallas import tpu as pltpu
from jax.sharding import PartitionSpec as P

F32 = jnp.float32
BF16 = jnp.bfloat16
MESH = pl.DeviceIdType.MESH
COLS = 128
UNIT = 8
PER_ROW = COLS // UNIT


def rms_norm(wide, gain):
    scale = lax.rsqrt(jnp.mean(wide * wide, axis=-1, keepdims=True) + 1e-06)
    return wide * scale * gain


def silu(v):
    return v / (1.0 + jnp.exp(-v))


def column_sum(total):
    width, chans = (COLS - UNIT, total.shape[1] // 3)
    left = pltpu.roll(total[:, :chans], 1, 0)
    right = pltpu.roll(total[:, 2 * chans :], COLS - 1, 0)
    return (left + total[:, chans : 2 * chans] + right)[:width]


def padded(value):
    return jnp.concatenate([value, jnp.zeros((COLS - value.shape[0], value.shape[1]), F32)], axis=0)


def taps_of(weight, pairs):
    return jnp.concatenate(
        [jnp.concatenate([weight[a, b, e] for e in range(3)], axis=1) for a, b in pairs], axis=0
    )


def cells_of(field, frame, pairs, rows):
    return jnp.concatenate(
        [
            jnp.concatenate([field[frame + a, row + b] for row in rows], axis=0)
            for a, b in pairs
        ],
        axis=1,
    )


def kernel(
    steps,
    blocks,
    video_hbm,
    norm_gain_hbm,
    first_hbm,
    second_hbm,
    attn_gain_hbm,
    query_hbm,
    key_hbm,
    value_hbm,
    out_hbm,
    result_ref,
    video,
    norm_gain,
    first,
    second,
    attn_gain,
    query_w,
    key_w,
    value_w,
    out_w,
    act,
    mid,
    acc,
    hidden,
    gathered,
    answer,
    returned,
    load_sem,
    halo_send,
    halo_recv,
    swap_send,
    swap_recv,
):
    t, r = (lax.axis_index("tm"), lax.axis_index("rows"))
    chans = video.shape[-1]
    loads = [
        pltpu.make_async_copy(src, dst, load_sem.at[i])
        for i, (src, dst) in enumerate(
            [
                (video_hbm, video),
                (norm_gain_hbm, norm_gain),
                (first_hbm, first),
                (second_hbm, second),
                (attn_gain_hbm, attn_gain),
                (query_hbm, query_w),
                (key_hbm, key_w),
                (value_hbm, value_w),
                (out_hbm, out_w),
            ]
        )
    ]
    for load in loads:
        load.start()

    has_next, has_prev = (t < steps - 1, t > 0)
    has_above, has_below = (r < blocks - 1, r > 0)

    barrier = pltpu.get_barrier_semaphore()

    def greet(j, _):
        peer = lax.rem(t + j, steps)
        pl.semaphore_signal(barrier, inc=1, device_id={"tm": peer, "rows": r}, device_id_type=MESH)
        return 0

    lax.fori_loop(1, steps, greet, 0)

    @pl.when(has_above)
    def _():
        pl.semaphore_signal(barrier, inc=1, device_id={"tm": t, "rows": r + 1}, device_id_type=MESH)

    @pl.when(has_below)
    def _():
        pl.semaphore_signal(barrier, inc=1, device_id={"tm": t, "rows": r - 1}, device_id_type=MESH)

    for field in (act, mid):

        @pl.when(t == 0)
        def _(field=field):
            field[0:2] = jnp.zeros((2,) + field.shape[1:], BF16)

        @pl.when(r == 0)
        def _(field=field):
            for frame in range(4):
                field[frame, 0] = jnp.zeros((COLS, chans), BF16)

        @pl.when(r == blocks - 1)
        def _(field=field):
            for frame in range(4):
                field[frame, 5] = jnp.zeros((COLS, chans), BF16)

    loads[0].wait()
    loads[1].wait()
    gain = norm_gain[...].astype(F32)
    for frame in range(2):
        for row in range(4):
            wide = video[frame, row].astype(F32)
            act[frame + 2, row + 1] = padded(silu(rms_norm(wide, gain))).astype(BF16)

    pl.semaphore_wait(
        barrier, steps - 1 + has_above.astype(jnp.int32) + has_below.astype(jnp.int32)
    )

    def halo(which, field, slot, src, dst, device):
        return pltpu.make_async_remote_copy(
            src_ref=field.at[src],
            dst_ref=field.at[dst],
            send_sem=halo_send.at[which, slot],
            recv_sem=halo_recv.at[which, slot],
            device_id=device,
            device_id_type=MESH,
        )

    own, past = (pl.ds(2, 2), pl.ds(0, 2))

    def copies(which, field):
        later = {"tm": jnp.minimum(t + 1, steps - 1), "rows": r}
        above = {"tm": t, "rows": jnp.minimum(r + 1, blocks - 1)}
        below = {"tm": t, "rows": jnp.maximum(r - 1, 0)}
        return {
            "inner": halo(which, field, 0, (own, pl.ds(2, 2)), (past, pl.ds(2, 2)), later),
            "low": halo(which, field, 1, (own, 1), (past, 1), later),
            "high": halo(which, field, 2, (own, 4), (past, 4), later),
            "up": halo(which, field, 3, (own, 4), (own, 0), above),
            "down": halo(which, field, 4, (own, 1), (own, 5), below),
            "on_low": halo(which, field, 5, (own, 0), (past, 0), later),
            "on_high": halo(which, field, 6, (own, 5), (past, 5), later),
        }

    def when(flag, action):
        pl.when(flag)(action)

    def local_part(field, weight):
        for frame in range(2):
            early = range(2 - frame, 3)
            for rows, span in (((1, 2), (0, 1, 2)), ((0,), (1, 2)), ((3,), (0, 1))):
                pairs = [(a, b) for a in early for b in span]
                total = jnp.dot(
                    cells_of(field, frame, pairs, rows),
                    taps_of(weight, pairs),
                    preferred_element_type=F32,
                )
                for i, row in enumerate(rows):
                    acc[frame, row] = total[i * COLS : (i + 1) * COLS]

    def past_part(field, weight, parts, finish):
        for frame in range(2):
            early = range(0, 2 - frame)
            for rows, span in parts:
                pairs = [(a, b) for a in early for b in span]
                total = jnp.dot(
                    cells_of(field, frame, pairs, rows),
                    taps_of(weight, pairs),
                    preferred_element_type=F32,
                )
                for i, row in enumerate(rows):
                    part = acc[frame, row] + total[i * COLS : (i + 1) * COLS]
                    if finish is None:
                        acc[frame, row] = part
                    else:
                        finish(frame, row, part)

    def edge_part(field, weight, finish):
        for frame in range(2):
            for row, b in ((0, 0), (3, 2)):
                pairs = [(a, b) for a in range(3)]
                total = jnp.dot(
                    cells_of(field, frame, pairs, (row,)),
                    taps_of(weight, pairs),
                    preferred_element_type=F32,
                )
                finish(frame, row, acc[frame, row] + total)

    inner_rows = (((1, 2), (0, 1, 2)),)
    outer_rows = (((0,), (1, 2)), ((3,), (0, 1)))

    def to_mid(frame, row, total):
        mid[frame + 2, row + 1] = padded(silu(column_sum(total))).astype(BF16)

    def to_hidden(frame, row, total):
        acc[frame, row, :, 0:chans] = padded(
            video[frame, row].astype(F32) + column_sum(total)
        )

    def pack_hidden(rows):
        for row in rows:
            one, two = (
                acc[frame, row, :, 0:chans].reshape(PER_ROW, UNIT, chans) for frame in range(2)
            )
            hidden[row] = jnp.concatenate([one, two], axis=1).astype(BF16)

    chunk_rows = ((1, 2), (0, 3))

    def unit_of(chunk, peer):
        half = peer // PER_ROW
        first_row, second_row = chunk_rows[chunk]
        return (first_row + half * (second_row - first_row), lax.rem(peer, PER_ROW))

    def forth(chunk, peer):
        row, place = unit_of(chunk, peer)
        return pltpu.make_async_remote_copy(
            src_ref=hidden.at[row, place],
            dst_ref=gathered.at[chunk, t],
            send_sem=swap_send.at[0, chunk],
            recv_sem=swap_recv.at[0, chunk],
            device_id={"tm": peer, "rows": r},
            device_id_type=MESH,
        )

    def back(chunk, peer):
        return pltpu.make_async_remote_copy(
            src_ref=answer.at[chunk, peer],
            dst_ref=returned.at[chunk, t],
            send_sem=swap_send.at[1, chunk],
            recv_sem=swap_recv.at[1, chunk],
            device_id={"tm": peer, "rows": r},
            device_id_type=MESH,
        )

    def send_all(make, chunk):
        def body(j, _):
            make(chunk, lax.rem(t + j, steps)).start()
            return 0

        lax.fori_loop(1, steps, body, 0)

    def scatter(chunk):
        send_all(forth, chunk)
        row, place = unit_of(chunk, t)
        pltpu.make_async_copy(
            hidden.at[row, place], gathered.at[chunk, t], swap_recv.at[0, chunk]
        ).start()

    def attend(chunk):
        pltpu.make_async_copy(
            gathered.at[chunk], gathered.at[chunk], swap_recv.at[0, chunk]
        ).wait()
        cells = steps * 2 * UNIT
        wide = gathered[chunk].reshape(cells, chans).astype(F32)
        normed = rms_norm(wide, attn_gain[...].astype(F32)).astype(BF16)
        joined = jnp.concatenate([query_w[...], key_w[...], value_w[...]], axis=1)
        projected = jnp.dot(normed, joined, preferred_element_type=F32).astype(BF16)
        query = projected[:, :chans]
        key = projected[:, chans : 2 * chans]
        value = projected[:, 2 * chans :]
        tile = 128
        spot = lax.broadcasted_iota(jnp.int32, (tile, tile), 0)
        other = lax.broadcasted_iota(jnp.int32, (tile, tile), 1)
        same = lax.rem(spot, UNIT) == lax.rem(other, UNIT)
        causal = same & (other <= spot)
        root = 1.0 / jnp.sqrt(F32(chans))
        for i in range(cells // tile):
            rows = slice(i * tile, (i + 1) * tile)
            scores = lax.dot_general(
                query[rows],
                key[: (i + 1) * tile],
                (((1,), (1,)), ((), ())),
                preferred_element_type=F32,
            ) * root
            tiles = [
                jnp.where(
                    causal if j == i else same, scores[:, j * tile : (j + 1) * tile], F32(-1e30)
                )
                for j in range(i + 1)
            ]
            top = jnp.max(functools.reduce(jnp.maximum, tiles), axis=1, keepdims=True)
            weights = [jnp.exp(part - top) for part in tiles]
            total = jnp.sum(functools.reduce(jnp.add, weights), axis=1, keepdims=True)
            mixed = jnp.dot(
                jnp.concatenate([part.astype(BF16) for part in weights], axis=1),
                value[: (i + 1) * tile],
                preferred_element_type=F32,
            )
            mixed = (mixed / total).astype(BF16)
            shown = wide[rows] + jnp.dot(mixed, out_w[...], preferred_element_type=F32)
            count = tile // (2 * UNIT)
            answer[chunk, i * count : (i + 1) * count] = (
                shown.astype(BF16).reshape(count, 2 * UNIT, chans)
            )
        send_all(back, chunk)
        pltpu.make_async_copy(
            answer.at[chunk, t], returned.at[chunk, t], swap_recv.at[1, chunk]
        ).start()

    def collect(chunk):
        pltpu.make_async_copy(
            returned.at[chunk], returned.at[chunk], swap_recv.at[1, chunk]
        ).wait()
        for half, row in enumerate(chunk_rows[chunk]):
            units = returned[chunk, half * PER_ROW : (half + 1) * PER_ROW].astype(F32)
            for frame in range(2):
                part = units[:, frame * UNIT : (frame + 1) * UNIT].reshape(COLS, chans)
                result_ref[frame, row] = part[: COLS - UNIT].astype(BF16)

    one = copies(0, act)
    when(has_above, one["up"].start)
    when(has_below, one["down"].start)
    for name in ("inner", "low", "high"):
        when(has_next, one[name].start)
    loads[2].wait()
    local_part(act, first)
    for name in ("inner", "low", "high"):
        when(has_prev, one[name].wait_recv)
    two = copies(1, mid)
    past_part(act, first, inner_rows, to_mid)
    when(has_next, two["inner"].start)
    past_part(act, first, outer_rows, None)

    def pass_on(copy):
        when(has_below, copy["up"].wait_recv)
        when(has_below & has_next, copy["on_low"].start)
        when(has_above, copy["down"].wait_recv)
        when(has_above & has_next, copy["on_high"].start)

    def passed_on(copy):
        when(has_below & has_prev, copy["on_low"].wait_recv)
        when(has_above & has_prev, copy["on_high"].wait_recv)

    pass_on(one)
    passed_on(one)
    edge_part(act, first, to_mid)

    when(has_above, two["up"].start)
    when(has_below, two["down"].start)
    for name in ("low", "high"):
        when(has_next, two[name].start)
    loads[3].wait()
    local_part(mid, second)
    for name in ("inner", "low", "high"):
        when(has_prev, two[name].wait_recv)
    past_part(mid, second, inner_rows, to_hidden)
    pack_hidden((1, 2))
    scatter(0)
    past_part(mid, second, outer_rows, None)
    pass_on(two)
    passed_on(two)
    edge_part(mid, second, to_hidden)
    pack_hidden((0, 3))
    scatter(1)

    for load in loads[4:]:
        load.wait()
    attend(0)
    attend(1)
    collect(0)
    collect(1)

    for copy in (one, two):
        when(has_above, copy["up"].wait_send)
        when(has_below, copy["down"].wait_send)
        for name in ("inner", "low", "high"):
            when(has_next, copy[name].wait_send)
        when(has_below & has_next, copy["on_low"].wait_send)
        when(has_above & has_next, copy["on_high"].wait_send)
    for way in range(2):
        for chunk in range(2):
            sent = gathered.at[chunk, pl.ds(0, steps - 1)]
            pltpu.make_async_copy(sent, sent, swap_send.at[way, chunk]).wait()


def local(video, norm_gain, first, second, attn_gain, query_w, key_w, value_w, out_w):
    steps, blocks = (lax.axis_size("tm"), lax.axis_size("rows"))
    frames, height, width, chans = video.shape
    anywhere = pl.BlockSpec(memory_space=pl.ANY)
    square = (chans, chans)
    return pl.pallas_call(
        functools.partial(kernel, steps, blocks),
        out_shape=jax.ShapeDtypeStruct(video.shape, video.dtype),
        in_specs=[anywhere] * 9,
        out_specs=pl.BlockSpec(memory_space=pltpu.VMEM),
        scratch_shapes=[
            pltpu.VMEM(video.shape, BF16),
            pltpu.VMEM((1, chans), BF16),
            pltpu.VMEM((3, 3, 3) + square, BF16),
            pltpu.VMEM((3, 3, 3) + square, BF16),
            pltpu.VMEM((1, chans), BF16),
            pltpu.VMEM(square, BF16),
            pltpu.VMEM(square, BF16),
            pltpu.VMEM(square, BF16),
            pltpu.VMEM(square, BF16),
            pltpu.VMEM((4, 6, COLS, chans), BF16),
            pltpu.VMEM((4, 6, COLS, chans), BF16),
            pltpu.VMEM((2, 4, COLS, 3 * chans), F32),
            pltpu.VMEM((4, PER_ROW, 2 * UNIT, chans), BF16),
            pltpu.VMEM((2, steps, 2 * UNIT, chans), BF16),
            pltpu.VMEM((2, steps, 2 * UNIT, chans), BF16),
            pltpu.VMEM((2, steps, 2 * UNIT, chans), BF16),
            pltpu.SemaphoreType.DMA((9,)),
            pltpu.SemaphoreType.DMA((2, 7)),
            pltpu.SemaphoreType.DMA((2, 7)),
            pltpu.SemaphoreType.DMA((2, 2)),
            pltpu.SemaphoreType.DMA((2, 2)),
        ],
        compiler_params=pltpu.CompilerParams(
            collective_id=0, has_side_effects=True, vmem_limit_bytes=56 * 1024 * 1024
        ),
    )(
        video,
        norm_gain.reshape(1, chans),
        first,
        second,
        attn_gain.reshape(1, chans),
        query_w,
        key_w,
        value_w,
        out_w,
    )


def solution(mesh):
    return jax.shard_map(
        local,
        mesh=mesh,
        in_specs=(P("tm", "rows", None, None), P(), P(), P(), P(), P(), P(), P(), P()),
        out_specs=P("tm", "rows", None, None),
        check_vma=False,
    )
```

time: 248 us -> 52.4 us (0.21)
  the two profiles are of different devices: /device:TPU:1 before, /device:TPU:353 now
where the time goes in v1:
time: 52.4 us; the launch traced here: 52.2 us
  Pallas kernels  50.6 us (97%)
  local copies, waits for them, and re-layouts  1.66 us (3%)
    pallas_call x1, Pallas kernels, local(): pl.pallas_call(functools.partial(kernel, steps, blocks), out_shape=jax.Sh...  50.6 us
    unnamed x1, local copies, waits for them, and re-layouts  1.66 us

profile of v1, /device:TPU:353, one launch (start us, length us, event | category | flops | bytes accessed | tf_op | source)
XLA Modules:
  0.0 52.2 jit_solution(8327744316311126949)
XLA Ops:
  0.0 50.6 %shard_map.91 = bf16[2,4,120,128]{3,2,1,0:T(8,128)(2,1)} custom-call(bf16[2,4,120,128]{3,2,1,0:T(8,128)(2,1)} %video_hbm.1, bf16[1,128]{1,0:T(2,128)(2,1)} %bitcast.2, bf16[3,3,3,128,128]{4,3,2,1,0:T(8,128)(2,1)} %first_hbm.1, bf16[3,3,3,128,128]{4,3,2,1,0:T(8,128)(2,1)} %second_hbm.1, bf16[1,128]{1,0:T(2,128)(2,1)} %bitcast.3, bf16[128,128]{1,0:T(8,128)(2,1)} %query_hbm.1, ...), custom_call_target="tpu_custom_call" | custom-call | tf_op jit(solution)/shard_map/pallas_call | solution.py:420
  50.6 1.7 %copy.11 = bf16[2,4,120,128]{3,2,1,0:T(8,128)(2,1)} copy(bf16[2,4,120,128]{3,2,1,0:T(8,128)(2,1)} %shard_map.91) | data formatting | bytes 491520

commit v2 on v1

v2 whole, which is shorter than its diff:
```python
import functools

import jax
import jax.numpy as jnp
from jax import lax
from jax.experimental import pallas as pl
from jax.experimental.pallas import tpu as pltpu
from jax.sharding import PartitionSpec as P

F32 = jnp.float32
BF16 = jnp.bfloat16
MESH = pl.DeviceIdType.MESH
COLS = 128
UNIT = 8
PER_ROW = COLS // UNIT


def rms_norm(wide, gain):
    scale = lax.rsqrt(jnp.mean(wide * wide, axis=-1, keepdims=True) + 1e-06)
    return wide * scale * gain


def silu(v):
    return v / (1.0 + jnp.exp(-v))


def column_sum(total):
    width, chans = (COLS - UNIT, total.shape[1] // 3)
    left = pltpu.roll(total[:, :chans], 1, 0)
    right = pltpu.roll(total[:, 2 * chans :], COLS - 1, 0)
    return (left + total[:, chans : 2 * chans] + right)[:width]


def padded(value):
    return jnp.concatenate([value, jnp.zeros((COLS - value.shape[0], value.shape[1]), F32)], axis=0)


def kernel(
    steps,
    blocks,
    video_hbm,
    norm_gain_hbm,
    first_hbm,
    second_hbm,
    attn_gain_hbm,
    query_hbm,
    key_hbm,
    value_hbm,
    out_hbm,
    result_ref,
    video,
    norm_gain,
    first,
    second,
    attn_gain,
    query_w,
    key_w,
    value_w,
    out_w,
    act,
    mid,
    acc,
    hidden,
    gathered,
    answer,
    returned,
    load_sem,
    halo_send,
    halo_recv,
    swap_send,
    swap_recv,
):
    t, r = (lax.axis_index("tm"), lax.axis_index("rows"))
    chans = video.shape[-1]
    loads = [
        pltpu.make_async_copy(src, dst, load_sem.at[i])
        for i, (src, dst) in enumerate(
            [
                (video_hbm, video),
                (norm_gain_hbm, norm_gain),
                (first_hbm, first),
                (second_hbm, second),
                (attn_gain_hbm, attn_gain),
                (query_hbm, query_w),
                (key_hbm, key_w),
                (value_hbm, value_w),
                (out_hbm, out_w),
            ]
        )
    ]
    for load in loads:
        load.start()

    has_next, has_prev = (t < steps - 1, t > 0)
    has_above, has_below = (r < blocks - 1, r > 0)

    barrier = pltpu.get_barrier_semaphore()

    def greet(j, _):
        peer = lax.rem(t + j, steps)
        pl.semaphore_signal(barrier, inc=1, device_id={"tm": peer, "rows": r}, device_id_type=MESH)
        return 0

    lax.fori_loop(1, steps, greet, 0)

    @pl.when(has_above)
    def _():
        pl.semaphore_signal(barrier, inc=1, device_id={"tm": t, "rows": r + 1}, device_id_type=MESH)

    @pl.when(has_below)
    def _():
        pl.semaphore_signal(barrier, inc=1, device_id={"tm": t, "rows": r - 1}, device_id_type=MESH)

    flip = (lax.rem(r, 4) < 2).astype(jnp.int32)

    def place(q):
        return q + flip * (3 - 2 * q)

    def line(q):
        return q + 1 + flip * (3 - 2 * q)

    def tap(b):
        return b + flip * (2 - 2 * b)

    for field in (act, mid):

        @pl.when(t == 0)
        def _(field=field):
            field[0:2] = jnp.zeros((2,) + field.shape[1:], BF16)

        @pl.when(r == 0)
        def _(field=field):
            for frame in range(4):
                field[frame, 0] = jnp.zeros((COLS, chans), BF16)

        @pl.when(r == blocks - 1)
        def _(field=field):
            for frame in range(4):
                field[frame, 5] = jnp.zeros((COLS, chans), BF16)

    loads[0].wait()
    loads[1].wait()
    gain = norm_gain[...].astype(F32)
    for frame in range(2):
        for row in range(4):
            wide = video[frame, row].astype(F32)
            act[frame + 2, row + 1] = padded(silu(rms_norm(wide, gain))).astype(BF16)

    pl.semaphore_wait(
        barrier, steps - 1 + has_above.astype(jnp.int32) + has_below.astype(jnp.int32)
    )

    def halo(which, field, slot, src, dst, device):
        return pltpu.make_async_remote_copy(
            src_ref=field.at[src],
            dst_ref=field.at[dst],
            send_sem=halo_send.at[which, slot],
            recv_sem=halo_recv.at[which, slot],
            device_id=device,
            device_id_type=MESH,
        )

    own, past = (pl.ds(2, 2), pl.ds(0, 2))
    has_near = jnp.where(flip == 1, has_above, has_below)
    has_far = jnp.where(flip == 1, has_below, has_above)

    def copies(which, field):
        later = {"tm": jnp.minimum(t + 1, steps - 1), "rows": r}
        near = {"tm": t, "rows": jnp.clip(r - 1 + 2 * flip, 0, blocks - 1)}
        far = {"tm": t, "rows": jnp.clip(r + 1 - 2 * flip, 0, blocks - 1)}
        onward, backward = (5 * flip, 5 - 5 * flip)
        return {
            "inner": halo(which, field, 0, (own, pl.ds(2, 2)), (past, pl.ds(2, 2)), later),
            "first": halo(which, field, 1, (own, line(0)), (past, line(0)), later),
            "last": halo(which, field, 2, (own, line(3)), (past, line(3)), later),
            "to_near": halo(which, field, 4 - flip, (own, line(0)), (own, backward), near),
            "to_far": halo(which, field, 3 + flip, (own, line(3)), (own, onward), far),
            "from_near": halo(which, field, 3 + flip, (own, line(0)), (own, onward), near),
            "from_far": halo(which, field, 4 - flip, (own, line(3)), (own, backward), far),
            "on_near": halo(which, field, 5, (own, onward), (past, onward), later),
            "on_far": halo(which, field, 6, (own, backward), (past, backward), later),
        }

    def when(flag, action):
        pl.when(flag)(action)

    def product(field, weight, frame, early, rows, span):
        pairs = [(a, b) for a in early for b in span]
        cells = jnp.concatenate(
            [
                jnp.concatenate([field[frame + a, line(q + b - 1)] for q in rows], axis=0)
                for a, b in pairs
            ],
            axis=1,
        )
        taps = jnp.concatenate(
            [
                jnp.concatenate([weight[a, tap(b), e] for e in range(3)], axis=1)
                for a, b in pairs
            ],
            axis=0,
        )
        return jnp.dot(cells, taps, preferred_element_type=F32)

    def part(total, i):
        return total[i * COLS : (i + 1) * COLS]

    every = (0, 1, 2)
    groups = (((1, 2), every), ((0,), (1, 2)), ((3,), (0, 1)))

    def to_mid(frame, q, total):
        mid[frame + 2, line(q)] = padded(silu(column_sum(total))).astype(BF16)

    def to_hidden(q, totals):
        one, two = (
            padded(video[frame, place(q)].astype(F32) + column_sum(total)).reshape(
                PER_ROW, UNIT, chans
            )
            for frame, total in enumerate(totals)
        )
        hidden[q] = jnp.concatenate([one, two], axis=1).astype(BF16)

    parity = lax.rem(t, 2)

    def peer_copy(src, dst, send, recv, peer):
        return pltpu.make_async_remote_copy(
            src_ref=src,
            dst_ref=dst,
            send_sem=send,
            recv_sem=recv,
            device_id={"tm": peer, "rows": r},
            device_id_type=MESH,
        )

    def scatter_all():
        def body(j, _):
            peer = lax.rem(t + j, steps)
            peer_copy(
                hidden.at[peer // PER_ROW, lax.rem(peer, PER_ROW)],
                gathered.at[0, t],
                swap_send.at[0, 0],
                swap_recv.at[0, 0],
                peer,
            ).start()
            return 0

        lax.fori_loop(1, steps, body, 0)
        pltpu.make_async_copy(
            hidden.at[t // PER_ROW, lax.rem(t, PER_ROW)], gathered.at[0, t], swap_recv.at[0, 0]
        ).start()

    def scatter_half(odd):
        def send(j):
            spot = lax.rem(t // 2 + j, PER_ROW)
            peer_copy(
                hidden.at[2 + odd, spot],
                gathered.at[1, t],
                swap_send.at[0, 1 + odd],
                swap_recv.at[0, 1],
                2 * spot + odd,
            ).start()

        def body(j, _):
            send(j)
            return 0

        lax.fori_loop(1, PER_ROW, body, 0)
        pl.when(parity != odd)(lambda: send(0))
        pl.when(parity == odd)(
            pltpu.make_async_copy(
                hidden.at[2 + odd, t // 2], gathered.at[1, t], swap_recv.at[0, 1]
            ).start
        )

    def attend(slot):
        pltpu.make_async_copy(gathered.at[slot], gathered.at[slot], swap_recv.at[0, slot]).wait()
        cells = steps * 2 * UNIT
        wide = gathered[slot].reshape(cells, chans).astype(F32)
        normed = rms_norm(wide, attn_gain[...].astype(F32)).astype(BF16)
        joined = jnp.concatenate([query_w[...], key_w[...], value_w[...]], axis=1)
        projected = jnp.dot(normed, joined, preferred_element_type=F32).astype(BF16)
        query = projected[:, :chans]
        key = projected[:, chans : 2 * chans]
        value = projected[:, 2 * chans :]
        tile = 128
        spot = lax.broadcasted_iota(jnp.int32, (tile, tile), 0)
        other = lax.broadcasted_iota(jnp.int32, (tile, tile), 1)
        same = lax.rem(spot, UNIT) == lax.rem(other, UNIT)
        causal = same & (other <= spot)
        root = 1.0 / jnp.sqrt(F32(chans))
        for i in range(cells // tile):
            rows = slice(i * tile, (i + 1) * tile)
            scores = (
                lax.dot_general(
                    query[rows],
                    key[: (i + 1) * tile],
                    (((1,), (1,)), ((), ())),
                    preferred_element_type=F32,
                )
                * root
            )
            tiles = [
                jnp.where(
                    causal if j == i else same, scores[:, j * tile : (j + 1) * tile], F32(-1e30)
                )
                for j in range(i + 1)
            ]
            top = jnp.max(functools.reduce(jnp.maximum, tiles), axis=1, keepdims=True)
            weights = [jnp.exp(one - top) for one in tiles]
            total = jnp.sum(functools.reduce(jnp.add, weights), axis=1, keepdims=True)
            mixed = jnp.dot(
                jnp.concatenate([one.astype(BF16) for one in weights], axis=1),
                value[: (i + 1) * tile],
                preferred_element_type=F32,
            )
            mixed = (mixed / total).astype(BF16)
            shown = wide[rows] + jnp.dot(mixed, out_w[...], preferred_element_type=F32)
            count = tile // (2 * UNIT)
            answer[slot, i * count : (i + 1) * count] = shown.astype(BF16).reshape(
                count, 2 * UNIT, chans
            )
        if slot == 0:
            home = returned.at[t // PER_ROW, lax.rem(t, PER_ROW)]
            arrived = swap_recv.at[1, 0]
        else:
            home = returned.at[2 + parity, t // 2]
            arrived = swap_recv.at[1, 1 + parity]

        def body(j, _):
            peer = lax.rem(t + j, steps)
            peer_copy(answer.at[slot, peer], home, swap_send.at[1, slot], arrived, peer).start()
            return 0

        lax.fori_loop(1, steps, body, 0)
        pltpu.make_async_copy(answer.at[slot, t], home, arrived).start()

    def collect(index, rows):
        block = returned.at[pl.ds(rows[0], len(rows))]
        pltpu.make_async_copy(block, block, swap_recv.at[1, index]).wait()
        for q in rows:
            units = returned[q].astype(F32)
            for frame in range(2):
                cols = units[:, frame * UNIT : (frame + 1) * UNIT].reshape(COLS, chans)
                result_ref[frame, place(q)] = cols[: COLS - UNIT].astype(BF16)

    one, two = (copies(0, act), copies(1, mid))
    when(has_far, one["to_far"].start)
    when(has_near, one["to_near"].start)
    for name in ("inner", "first", "last"):
        when(has_next, one[name].start)
    loads[2].wait()
    for frame in range(2):
        for rows, span in groups:
            total = product(act, first, frame, range(2 - frame, 3), rows, span)
            for i, q in enumerate(rows):
                acc[frame, q] = part(total, i)
    for name in ("inner", "first", "last"):
        when(has_prev, one[name].wait_recv)
    for rows, span in groups:
        for frame in range(2):
            total = product(act, first, frame, range(0, 2 - frame), rows, span)
            for i, q in enumerate(rows):
                if len(rows) == 2:
                    to_mid(frame, q, acc[frame, q] + part(total, i))
                else:
                    acc[frame, q] += part(total, i)
        if len(rows) == 2:
            when(has_next, two["inner"].start)

    def edge(field, weight, q):
        return [
            acc[frame, q] + product(field, weight, frame, every, (q,), (0,) if q == 0 else (2,))
            for frame in range(2)
        ]

    def take(copy, side, present):
        when(present, copy["from_" + side].wait_recv)
        when(present & has_next, copy["on_" + side].start)

    def taken(copy, side, present):
        when(present & has_prev, copy["on_" + side].wait_recv)

    take(one, "near", has_near)
    taken(one, "near", has_near)
    for frame, total in enumerate(edge(act, first, 0)):
        to_mid(frame, 0, total)
    when(has_near, two["to_near"].start)
    when(has_next, two["first"].start)
    take(one, "far", has_far)
    taken(one, "far", has_far)
    for frame, total in enumerate(edge(act, first, 3)):
        to_mid(frame, 3, total)
    when(has_far, two["to_far"].start)
    when(has_next, two["last"].start)

    loads[3].wait()
    for name in ("inner", "first"):
        when(has_prev, two[name].wait_recv)
    to_hidden(1, [product(mid, second, frame, every, (1,), every) for frame in range(2)])
    for frame in range(2):
        acc[frame, 0] = product(mid, second, frame, every, (0,), (1, 2))
    take(two, "near", has_near)
    when(has_prev, two["last"].wait_recv)
    to_hidden(2, [product(mid, second, frame, every, (2,), every) for frame in range(2)])
    taken(two, "near", has_near)
    to_hidden(0, edge(mid, second, 0))
    scatter_all()
    scatter_half(0)
    for frame in range(2):
        acc[frame, 3] = product(mid, second, frame, every, (3,), (0, 1))
    take(two, "far", has_far)
    taken(two, "far", has_far)
    to_hidden(3, edge(mid, second, 3))
    scatter_half(1)

    for load in loads[4:]:
        load.wait()
    attend(0)
    attend(1)
    collect(0, (0, 1))
    collect(1, (2,))
    collect(2, (3,))

    for copy in (one, two):
        for side, present in (("near", has_near), ("far", has_far)):
            when(present, copy["to_" + side].wait_send)
            when(present & has_next, copy["on_" + side].wait_send)
        for name in ("inner", "first", "last"):
            when(has_next, copy[name].wait_send)

    def gone(count, sem):
        sent = gathered.at[0, pl.ds(0, count)]
        pltpu.make_async_copy(sent, sent, sem).wait()

    gone(steps - 1, swap_send.at[0, 0])
    for odd in range(2):
        pl.when(parity == odd)(lambda odd=odd: gone(PER_ROW - 1, swap_send.at[0, 1 + odd]))
        pl.when(parity != odd)(lambda odd=odd: gone(PER_ROW, swap_send.at[0, 1 + odd]))
    for slot in range(2):
        gone(steps - 1, swap_send.at[1, slot])


def local(video, norm_gain, first, second, attn_gain, query_w, key_w, value_w, out_w):
    steps, blocks = (lax.axis_size("tm"), lax.axis_size("rows"))
    frames, height, width, chans = video.shape
    anywhere = pl.BlockSpec(memory_space=pl.ANY)
    square = (chans, chans)
    return pl.pallas_call(
        functools.partial(kernel, steps, blocks),
        out_shape=jax.ShapeDtypeStruct(video.shape, video.dtype),
        in_specs=[anywhere] * 9,
        out_specs=pl.BlockSpec(memory_space=pltpu.VMEM),
        scratch_shapes=[
            pltpu.VMEM(video.shape, BF16),
            pltpu.VMEM((1, chans), BF16),
            pltpu.VMEM((3, 3, 3) + square, BF16),
            pltpu.VMEM((3, 3, 3) + square, BF16),
            pltpu.VMEM((1, chans), BF16),
            pltpu.VMEM(square, BF16),
            pltpu.VMEM(square, BF16),
            pltpu.VMEM(square, BF16),
            pltpu.VMEM(square, BF16),
            pltpu.VMEM((4, 6, COLS, chans), BF16),
            pltpu.VMEM((4, 6, COLS, chans), BF16),
            pltpu.VMEM((2, 4, COLS, 3 * chans), F32),
            pltpu.VMEM((4, PER_ROW, 2 * UNIT, chans), BF16),
            pltpu.VMEM((2, steps, 2 * UNIT, chans), BF16),
            pltpu.VMEM((2, steps, 2 * UNIT, chans), BF16),
            pltpu.VMEM((4, PER_ROW, 2 * UNIT, chans), BF16),
            pltpu.SemaphoreType.DMA((9,)),
            pltpu.SemaphoreType.DMA((2, 7)),
            pltpu.SemaphoreType.DMA((2, 7)),
            pltpu.SemaphoreType.DMA((2, 3)),
            pltpu.SemaphoreType.DMA((2, 3)),
        ],
        compiler_params=pltpu.CompilerParams(
            collective_id=0, has_side_effects=True, vmem_limit_bytes=56 * 1024 * 1024
        ),
    )(
        video,
        norm_gain.reshape(1, chans),
        first,
        second,
        attn_gain.reshape(1, chans),
        query_w,
        key_w,
        value_w,
        out_w,
    )


def solution(mesh):
    return jax.shard_map(
        local,
        mesh=mesh,
        in_specs=(P("tm", "rows", None, None), P(), P(), P(), P(), P(), P(), P(), P()),
        out_specs=P("tm", "rows", None, None),
        check_vma=False,
    )
```

time: 52.4 us -> 51.8 us (0.989)
  the two profiles are of different devices: /device:TPU:353 before, /device:TPU:135 now
where the time goes in v2:
time: 51.8 us; the launch traced here: 51.6 us
  Pallas kernels  50 us (97%)
  local copies, waits for them, and re-layouts  1.66 us (3%)
    pallas_call x1, Pallas kernels, local(): pl.pallas_call(functools.partial(kernel, steps, blocks), out_shape=jax.Sh...  50 us
    unnamed x1, local copies, waits for them, and re-layouts  1.66 us

profile of v2, /device:TPU:135, one launch (start us, length us, event | category | flops | bytes accessed | tf_op | source)
XLA Modules:
  0.0 51.6 jit_solution(13264650150610754663)
XLA Ops:
  0.0 50.0 %shard_map.91 = bf16[2,4,120,128]{3,2,1,0:T(8,128)(2,1)} custom-call(bf16[2,4,120,128]{3,2,1,0:T(8,128)(2,1)} %video_hbm.1, bf16[1,128]{1,0:T(2,128)(2,1)} %bitcast.2, bf16[3,3,3,128,128]{4,3,2,1,0:T(8,128)(2,1)} %first_hbm.1, bf16[3,3,3,128,128]{4,3,2,1,0:T(8,128)(2,1)} %second_hbm.1, bf16[1,128]{1,0:T(2,128)(2,1)} %bitcast.3, bf16[128,128]{1,0:T(8,128)(2,1)} %query_hbm.1, ...), custom_call_target="tpu_custom_call" | custom-call | tf_op jit(solution)/shard_map/pallas_call | solution.py:448
  50.0 1.7 %copy.11 = bf16[2,4,120,128]{3,2,1,0:T(8,128)(2,1)} copy(bf16[2,4,120,128]{3,2,1,0:T(8,128)(2,1)} %shard_map.91) | data formatting | bytes 491520

commit v3 on v2

--- a/solution.py
+++ b/solution.py
@@ -103,13 +103,16 @@
 
     lax.fori_loop(1, steps, greet, 0)
 
-    @pl.when(has_above)
-    def _():
-        pl.semaphore_signal(barrier, inc=1, device_id={"tm": t, "rows": r + 1}, device_id_type=MESH)
-
-    @pl.when(has_below)
-    def _():
-        pl.semaphore_signal(barrier, inc=1, device_id={"tm": t, "rows": r - 1}, device_id_type=MESH)
+    met = steps - 1
+    for side, there in ((1, has_above), (-1, has_below)):
+        for shift, then in ((0, True), (1, has_next), (-1, has_prev)):
+            present = there if shift == 0 else there & then
+            peer = {"tm": t + shift, "rows": r + side}
+            met = met + present.astype(jnp.int32)
+
+            @pl.when(present)
+            def _(peer=peer):
+                pl.semaphore_signal(barrier, inc=1, device_id=peer, device_id_type=MESH)
 
     flip = (lax.rem(r, 4) < 2).astype(jnp.int32)
 
@@ -117,7 +120,7 @@
         return q + flip * (3 - 2 * q)
 
     def line(q):
-        return q + 1 + flip * (3 - 2 * q)
+        return q + 2 + flip * (3 - 2 * q)
 
     def tap(b):
         return b + flip * (2 - 2 * b)
@@ -131,12 +134,12 @@
         @pl.when(r == 0)
         def _(field=field):
             for frame in range(4):
-                field[frame, 0] = jnp.zeros((COLS, chans), BF16)
+                field[frame, 1] = jnp.zeros((COLS, chans), BF16)
 
         @pl.when(r == blocks - 1)
         def _(field=field):
             for frame in range(4):
-                field[frame, 5] = jnp.zeros((COLS, chans), BF16)
+                field[frame, 6] = jnp.zeros((COLS, chans), BF16)
 
     loads[0].wait()
     loads[1].wait()
@@ -144,41 +147,56 @@
     for frame in range(2):
         for row in range(4):
             wide = video[frame, row].astype(F32)
-            act[frame + 2, row + 1] = padded(silu(rms_norm(wide, gain))).astype(BF16)
-
-    pl.semaphore_wait(
-        barrier, steps - 1 + has_above.astype(jnp.int32) + has_below.astype(jnp.int32)
-    )
-
-    def halo(which, field, slot, src, dst, device):
+            act[frame + 2, row + 2] = padded(silu(rms_norm(wide, gain))).astype(BF16)
+
+    pl.semaphore_wait(barrier, met)
+
+    def halo(which, field, slots, src, dst, device):
         return pltpu.make_async_remote_copy(
             src_ref=field.at[src],
             dst_ref=field.at[dst],
-            send_sem=halo_send.at[which, slot],
-            recv_sem=halo_recv.at[which, slot],
+            send_sem=halo_send.at[which, slots[0]],
+            recv_sem=halo_recv.at[which, slots[1]],
             device_id=device,
             device_id_type=MESH,
         )
 
     own, past = (pl.ds(2, 2), pl.ds(0, 2))
-    has_near = jnp.where(flip == 1, has_above, has_below)
     has_far = jnp.where(flip == 1, has_below, has_above)
+    slow = has_far & ((lax.rem(r, 4) == 0) | (lax.rem(r, 4) == 3))
+    fast = has_far & ~((lax.rem(r, 4) == 0) | (lax.rem(r, 4) == 3))
 
     def copies(which, field):
-        later = {"tm": jnp.minimum(t + 1, steps - 1), "rows": r}
-        near = {"tm": t, "rows": jnp.clip(r - 1 + 2 * flip, 0, blocks - 1)}
-        far = {"tm": t, "rows": jnp.clip(r + 1 - 2 * flip, 0, blocks - 1)}
-        onward, backward = (5 * flip, 5 - 5 * flip)
+        next_t = jnp.minimum(t + 1, steps - 1)
+        near_r = jnp.clip(r - 1 + 2 * flip, 0, blocks - 1)
+        far_r = jnp.clip(r + 1 - 2 * flip, 0, blocks - 1)
+        later, near, far, next_near, next_far = (
+            {"tm": a, "rows": b}
+            for a, b in ((next_t, r), (t, near_r), (t, far_r), (next_t, near_r), (next_t, far_r))
+        )
+        near_land, far_land = (6 - 5 * flip, 1 + 5 * flip)
+        far_in, far_in2 = (line(4), line(5))
+        inner = pl.ds(3, 2)
         return {
-            "inner": halo(which, field, 0, (own, pl.ds(2, 2)), (past, pl.ds(2, 2)), later),
-            "first": halo(which, field, 1, (own, line(0)), (past, line(0)), later),
-            "last": halo(which, field, 2, (own, line(3)), (past, line(3)), later),
-            "to_near": halo(which, field, 4 - flip, (own, line(0)), (own, backward), near),
-            "to_far": halo(which, field, 3 + flip, (own, line(3)), (own, onward), far),
-            "from_near": halo(which, field, 3 + flip, (own, line(0)), (own, onward), near),
-            "from_far": halo(which, field, 4 - flip, (own, line(3)), (own, backward), far),
-            "on_near": halo(which, field, 5, (own, onward), (past, onward), later),
-            "on_far": halo(which, field, 6, (own, backward), (past, backward), later),
+            "inner": halo(which, field, (0, 0), (own, inner), (past, inner), later),
+            "first": halo(which, field, (1, 1), (own, line(0)), (past, line(0)), later),
+            "last": halo(which, field, (2, 2), (own, line(3)), (past, line(3)), later),
+            "to_near": halo(which, field, (3, 4 - flip), (own, line(0)), (own, near_land), near),
+            "to_far": halo(which, field, (4, 3 + flip), (own, line(3)), (own, far_land), far),
+            "diag_near": halo(
+                which, field, (5, 6 - flip), (own, line(0)), (past, near_land), next_near
+            ),
+            "diag_far": halo(
+                which, field, (6, 5 + flip), (own, line(3)), (past, far_land), next_far
+            ),
+            "from_near": halo(which, field, (3, 3 + flip), (own, line(0)), (own, line(-1)), near),
+            "from_far": halo(which, field, (4, 4 - flip), (own, line(3)), (own, far_in), far),
+            "past_near": halo(which, field, (5, 5 + flip), (own, line(0)), (past, line(-1)), later),
+            "on_far": halo(which, field, (7, 6 - flip), (own, far_in), (past, far_in), later),
+            "to_far2": halo(which, field, (8, 7), (own, line(2)), (own, 7 * flip), far),
+            "from_far2": halo(which, field, (8, 7), (own, line(2)), (own, far_in2), far),
+            "on_far2": halo(which, field, (9, 8), (own, far_in2), (past, far_in2), later),
+            "beyond": halo(which, field, (9, 8), (own, far_in), (past, far_in), later),
         }
 
     def when(flag, action):
@@ -345,7 +363,10 @@
 
     one, two = (copies(0, act), copies(1, mid))
     when(has_far, one["to_far"].start)
-    when(has_near, one["to_near"].start)
+    one["to_near"].start()
+    when(has_next, one["diag_near"].start)
+    when(has_next & fast, one["diag_far"].start)
+    when(slow, one["to_far2"].start)
     for name in ("inner", "first", "last"):
         when(has_next, one[name].start)
     loads[2].wait()
@@ -373,24 +394,20 @@
             for frame in range(2)
         ]
 
-    def take(copy, side, present):
-        when(present, copy["from_" + side].wait_recv)
-        when(present & has_next, copy["on_" + side].start)
-
-    def taken(copy, side, present):
-        when(present & has_prev, copy["on_" + side].wait_recv)
-
-    take(one, "near", has_near)
-    taken(one, "near", has_near)
+    one["from_near"].wait_recv()
+    when(has_prev, one["past_near"].wait_recv)
     for frame, total in enumerate(edge(act, first, 0)):
         to_mid(frame, 0, total)
-    when(has_near, two["to_near"].start)
+    two["to_near"].start()
+    when(has_next, two["diag_near"].start)
     when(has_next, two["first"].start)
-    take(one, "far", has_far)
-    taken(one, "far", has_far)
+    when(has_far, one["from_far"].wait_recv)
+    when(has_next & slow, one["on_far"].start)
+    when(has_prev & has_far, one["on_far"].wait_recv)
     for frame, total in enumerate(edge(act, first, 3)):
         to_mid(frame, 3, total)
-    when(has_far, two["to_far"].start)
+    when(fast, two["to_far"].start)
+    when(has_next & fast, two["diag_far"].start)
     when(has_next, two["last"].start)
 
     loads[3].wait()
@@ -399,17 +416,28 @@
     to_hidden(1, [product(mid, second, frame, every, (1,), every) for frame in range(2)])
     for frame in range(2):
         acc[frame, 0] = product(mid, second, frame, every, (0,), (1, 2))
-    take(two, "near", has_near)
+    two["from_near"].wait_recv()
+    when(has_prev, two["past_near"].wait_recv)
+    to_hidden(0, edge(mid, second, 0))
+    scatter_all()
+
+    @pl.when(slow)
+    def _():
+        one["from_far2"].wait_recv()
+        when(has_next, one["on_far2"].start)
+        when(has_prev, one["on_far2"].wait_recv)
+        for frame in range(2):
+            to_mid(frame, 4, product(act, first, frame, every, (4,), every))
+        when(has_next, two["beyond"].start)
+
     when(has_prev, two["last"].wait_recv)
     to_hidden(2, [product(mid, second, frame, every, (2,), every) for frame in range(2)])
-    taken(two, "near", has_near)
-    to_hidden(0, edge(mid, second, 0))
-    scatter_all()
     scatter_half(0)
     for frame in range(2):
         acc[frame, 3] = product(mid, second, frame, every, (3,), (0, 1))
-    take(two, "far", has_far)
-    taken(two, "far", has_far)
+    when(fast, two["from_far"].wait_recv)
+    when(has_prev & fast, two["on_far"].wait_recv)
+    when(has_prev & slow, two["beyond"].wait_recv)
     to_hidden(3, edge(mid, second, 3))
     scatter_half(1)
 
@@ -422,11 +450,15 @@
     collect(2, (3,))
 
     for copy in (one, two):
-        for side, present in (("near", has_near), ("far", has_far)):
-            when(present, copy["to_" + side].wait_send)
-            when(present & has_next, copy["on_" + side].wait_send)
-        for name in ("inner", "first", "last"):
+        copy["to_near"].wait_send()
+        for name in ("inner", "first", "last", "diag_near"):
             when(has_next, copy[name].wait_send)
+        when(has_next & fast, copy["diag_far"].wait_send)
+    when(has_far, one["to_far"].wait_send)
+    when(fast, two["to_far"].wait_send)
+    when(slow, one["to_far2"].wait_send)
+    for copy in (one["on_far"], one["on_far2"], two["beyond"]):
+        when(has_next & slow, copy.wait_send)
 
     def gone(count, sem):
         sent = gathered.at[0, pl.ds(0, count)]
@@ -460,16 +492,16 @@
             pltpu.VMEM(square, BF16),
             pltpu.VMEM(square, BF16),
             pltpu.VMEM(square, BF16),
-            pltpu.VMEM((4, 6, COLS, chans), BF16),
-            pltpu.VMEM((4, 6, COLS, chans), BF16),
+            pltpu.VMEM((4, 8, COLS, chans), BF16),
+            pltpu.VMEM((4, 8, COLS, chans), BF16),
             pltpu.VMEM((2, 4, COLS, 3 * chans), F32),
             pltpu.VMEM((4, PER_ROW, 2 * UNIT, chans), BF16),
             pltpu.VMEM((2, steps, 2 * UNIT, chans), BF16),
             pltpu.VMEM((2, steps, 2 * UNIT, chans), BF16),
             pltpu.VMEM((4, PER_ROW, 2 * UNIT, chans), BF16),
             pltpu.SemaphoreType.DMA((9,)),
-            pltpu.SemaphoreType.DMA((2, 7)),
-            pltpu.SemaphoreType.DMA((2, 7)),
+            pltpu.SemaphoreType.DMA((2, 10)),
+            pltpu.SemaphoreType.DMA((2, 10)),
             pltpu.SemaphoreType.DMA((2, 3)),
             pltpu.SemaphoreType.DMA((2, 3)),
         ],

time: 51.8 us -> 54 us (1.042)
  Pallas kernels: 50 us -> 52.2 us
    pallas_call x1, Pallas kernels: 50 us -> 52.2 us  [local(): pl.pallas_call(functools.partial(kernel, steps, blocks), out_shape=jax.Sh...]
where the time goes in v3:
time: 54 us; the launch traced here: 53.8 us
  Pallas kernels  52.2 us (97%)
  local copies, waits for them, and re-layouts  1.66 us (3%)
    pallas_call x1, Pallas kernels, local(): pl.pallas_call(functools.partial(kernel, steps, blocks), out_shape=jax.Sh...  52.2 us
    unnamed x1, local copies, waits for them, and re-layouts  1.66 us

profile of v3, /device:TPU:135, one launch (start us, length us, event | category | flops | bytes accessed | tf_op | source)
XLA Modules:
  0.0 53.8 jit_solution(12395306135517495916)
XLA Ops:
  0.0 52.2 %shard_map.91 = bf16[2,4,120,128]{3,2,1,0:T(8,128)(2,1)} custom-call(bf16[2,4,120,128]{3,2,1,0:T(8,128)(2,1)} %video_hbm.1, bf16[1,128]{1,0:T(2,128)(2,1)} %bitcast.2, bf16[3,3,3,128,128]{4,3,2,1,0:T(8,128)(2,1)} %first_hbm.1, bf16[3,3,3,128,128]{4,3,2,1,0:T(8,128)(2,1)} %second_hbm.1, bf16[1,128]{1,0:T(2,128)(2,1)} %bitcast.3, bf16[128,128]{1,0:T(8,128)(2,1)} %query_hbm.1, ...), custom_call_target="tpu_custom_call" | custom-call | tf_op jit(solution)/shard_map/pallas_call | solution.py:480
  52.2 1.7 %copy.11 = bf16[2,4,120,128]{3,2,1,0:T(8,128)(2,1)} copy(bf16[2,4,120,128]{3,2,1,0:T(8,128)(2,1)} %shard_map.91) | data formatting | bytes 491520

commit v4 on v3

--- a/solution.py
+++ b/solution.py
@@ -64,9 +64,12 @@
     gathered,
     answer,
     returned,
+    relay,
     load_sem,
     halo_send,
     halo_recv,
+    relay_send,
+    relay_recv,
     swap_send,
     swap_recv,
 ):
@@ -114,6 +117,22 @@
             def _(peer=peer):
                 pl.semaphore_signal(barrier, inc=1, device_id=peer, device_id_type=MESH)
 
+    outer = (lax.rem(r, 4) == 0) | (lax.rem(r, 4) == 3)
+    mirror = r + 3 - 6 * (lax.rem(r, 4) == 3).astype(jnp.int32)
+    relays = [(t, r + 4, outer & (r < blocks - 4)), (t, r - 4, outer & (r > 3))]
+    relays += [
+        (t + shift, mirror, outer & then)
+        for shift, then in ((0, True), (1, has_next), (-1, has_prev))
+    ]
+    for to_t, to_r, present in relays:
+        met = met + present.astype(jnp.int32)
+
+        @pl.when(present)
+        def _(to_t=to_t, to_r=to_r):
+            pl.semaphore_signal(
+                barrier, inc=1, device_id={"tm": to_t, "rows": to_r}, device_id_type=MESH
+            )
+
     flip = (lax.rem(r, 4) < 2).astype(jnp.int32)
 
     def place(q):
@@ -163,8 +182,8 @@
 
     own, past = (pl.ds(2, 2), pl.ds(0, 2))
     has_far = jnp.where(flip == 1, has_below, has_above)
-    slow = has_far & ((lax.rem(r, 4) == 0) | (lax.rem(r, 4) == 3))
-    fast = has_far & ~((lax.rem(r, 4) == 0) | (lax.rem(r, 4) == 3))
+    slow, fast = (has_far & outer, has_far & ~outer)
+    relaying = outer & jnp.where(flip == 1, r < blocks - 4, r > 3)
 
     def copies(which, field):
         next_t = jnp.minimum(t + 1, steps - 1)
@@ -192,15 +211,42 @@
             "from_near": halo(which, field, (3, 3 + flip), (own, line(0)), (own, line(-1)), near),
             "from_far": halo(which, field, (4, 4 - flip), (own, line(3)), (own, far_in), far),
             "past_near": halo(which, field, (5, 5 + flip), (own, line(0)), (past, line(-1)), later),
-            "on_far": halo(which, field, (7, 6 - flip), (own, far_in), (past, far_in), later),
-            "to_far2": halo(which, field, (8, 7), (own, line(2)), (own, 7 * flip), far),
+            "past_far": halo(which, field, (6, 6 - flip), (own, line(3)), (past, far_in), later),
             "from_far2": halo(which, field, (8, 7), (own, line(2)), (own, far_in2), far),
-            "on_far2": halo(which, field, (9, 8), (own, far_in2), (past, far_in2), later),
+            "past_far2": halo(which, field, (8, 8), (own, line(2)), (past, far_in2), later),
             "beyond": halo(which, field, (9, 8), (own, far_in), (past, far_in), later),
         }
 
+    def across(i):
+        return pltpu.make_async_remote_copy(
+            src_ref=act.at[own, line(3 - i)],
+            dst_ref=relay.at[i],
+            send_sem=relay_send.at[i],
+            recv_sem=relay_recv.at[i],
+            device_id={"tm": t, "rows": jnp.clip(r + 4 - 8 * flip, 0, blocks - 1)},
+            device_id_type=MESH,
+        )
+
+    def relayed(i, later):
+        return pltpu.make_async_remote_copy(
+            src_ref=relay.at[i],
+            dst_ref=act.at[past if later else own, 7 * flip if i else 1 + 5 * flip],
+            send_sem=relay_send.at[2 + 2 * i + later],
+            recv_sem=halo_recv.at[0, 7 + later if i else (5 if later else 3) + flip],
+            device_id={
+                "tm": jnp.minimum(t + later, steps - 1),
+                "rows": jnp.clip(mirror, 0, blocks - 1),
+            },
+            device_id_type=MESH,
+        )
+
     def when(flag, action):
         pl.when(flag)(action)
+
+    def pass_on(i):
+        when(relaying, across(i).wait_recv)
+        when(relaying, relayed(i, 0).start)
+        when(relaying & has_next, relayed(i, 1).start)
 
     def product(field, weight, frame, early, rows, span):
         pairs = [(a, b) for a in early for b in span]
@@ -362,11 +408,12 @@
                 result_ref[frame, place(q)] = cols[: COLS - UNIT].astype(BF16)
 
     one, two = (copies(0, act), copies(1, mid))
-    when(has_far, one["to_far"].start)
+    when(slow, across(0).start)
+    when(fast, one["to_far"].start)
     one["to_near"].start()
     when(has_next, one["diag_near"].start)
     when(has_next & fast, one["diag_far"].start)
-    when(slow, one["to_far2"].start)
+    when(slow, across(1).start)
     for name in ("inner", "first", "last"):
         when(has_next, one[name].start)
     loads[2].wait()
@@ -401,9 +448,9 @@
     two["to_near"].start()
     when(has_next, two["diag_near"].start)
     when(has_next, two["first"].start)
+    pass_on(0)
     when(has_far, one["from_far"].wait_recv)
-    when(has_next & slow, one["on_far"].start)
-    when(has_prev & has_far, one["on_far"].wait_recv)
+    when(has_prev & has_far, one["past_far"].wait_recv)
     for frame, total in enumerate(edge(act, first, 3)):
         to_mid(frame, 3, total)
     when(fast, two["to_far"].start)
@@ -421,11 +468,12 @@
     to_hidden(0, edge(mid, second, 0))
     scatter_all()
 
+    pass_on(1)
+
     @pl.when(slow)
     def _():
         one["from_far2"].wait_recv()
-        when(has_next, one["on_far2"].start)
-        when(has_prev, one["on_far2"].wait_recv)
+        when(has_prev, one["past_far2"].wait_recv)
         for frame in range(2):
             to_mid(frame, 4, product(act, first, frame, every, (4,), every))
         when(has_next, two["beyond"].start)
@@ -436,7 +484,7 @@
     for frame in range(2):
         acc[frame, 3] = product(mid, second, frame, every, (3,), (0, 1))
     when(fast, two["from_far"].wait_recv)
-    when(has_prev & fast, two["on_far"].wait_recv)
+    when(has_prev & fast, two["past_far"].wait_recv)
     when(has_prev & slow, two["beyond"].wait_recv)
     to_hidden(3, edge(mid, second, 3))
     scatter_half(1)
@@ -454,11 +502,12 @@
         for name in ("inner", "first", "last", "diag_near"):
             when(has_next, copy[name].wait_send)
         when(has_next & fast, copy["diag_far"].wait_send)
-    when(has_far, one["to_far"].wait_send)
-    when(fast, two["to_far"].wait_send)
-    when(slow, one["to_far2"].wait_send)
-    for copy in (one["on_far"], one["on_far2"], two["beyond"]):
-        when(has_next & slow, copy.wait_send)
+        when(fast, copy["to_far"].wait_send)
+    when(has_next & slow, two["beyond"].wait_send)
+    for i in range(2):
+        when(slow, across(i).wait_send)
+        when(relaying, relayed(i, 0).wait_send)
+        when(relaying & has_next, relayed(i, 1).wait_send)
 
     def gone(count, sem):
         sent = gathered.at[0, pl.ds(0, count)]
@@ -499,9 +548,12 @@
             pltpu.VMEM((2, steps, 2 * UNIT, chans), BF16),
             pltpu.VMEM((2, steps, 2 * UNIT, chans), BF16),
             pltpu.VMEM((4, PER_ROW, 2 * UNIT, chans), BF16),
+            pltpu.VMEM((2, 2, COLS, chans), BF16),
             pltpu.SemaphoreType.DMA((9,)),
             pltpu.SemaphoreType.DMA((2, 10)),
-            pltpu.SemaphoreType.DMA((2, 10)),
+            pltpu.SemaphoreType.DMA((2, 9)),
+            pltpu.SemaphoreType.DMA((6,)),
+            pltpu.SemaphoreType.DMA((2,)),
             pltpu.SemaphoreType.DMA((2, 3)),
             pltpu.SemaphoreType.DMA((2, 3)),
         ],

time: 54 us -> 59.3 us (1.098)
  Pallas kernels: 52.2 us -> 57.5 us
    pallas_call x1, Pallas kernels: 52.2 us -> 57.5 us  [local(): pl.pallas_call(functools.partial(kernel, steps, blocks), out_shape=jax.Sh...]
where the time goes in v4:
time: 59.3 us; the launch traced here: 59.2 us
  Pallas kernels  57.5 us (97%)
  local copies, waits for them, and re-layouts  1.66 us (3%)
    pallas_call x1, Pallas kernels, local(): pl.pallas_call(functools.partial(kernel, steps, blocks), out_shape=jax.Sh...  57.5 us
    unnamed x1, local copies, waits for them, and re-layouts  1.66 us

profile of v4, /device:TPU:135, one launch (start us, length us, event | category | flops | bytes accessed | tf_op | source)
XLA Modules:
  0.0 59.2 jit_solution(3528446321666655325)
XLA Ops:
  0.0 57.5 %shard_map.91 = bf16[2,4,120,128]{3,2,1,0:T(8,128)(2,1)} custom-call(bf16[2,4,120,128]{3,2,1,0:T(8,128)(2,1)} %video_hbm.1, bf16[1,128]{1,0:T(2,128)(2,1)} %bitcast.2, bf16[3,3,3,128,128]{4,3,2,1,0:T(8,128)(2,1)} %first_hbm.1, bf16[3,3,3,128,128]{4,3,2,1,0:T(8,128)(2,1)} %second_hbm.1, bf16[1,128]{1,0:T(2,128)(2,1)} %bitcast.3, bf16[128,128]{1,0:T(8,128)(2,1)} %query_hbm.1, ...), custom_call_target="tpu_custom_call" | custom-call | tf_op jit(solution)/shard_map/pallas_call | solution.py:529
  57.5 1.7 %copy.11 = bf16[2,4,120,128]{3,2,1,0:T(8,128)(2,1)} copy(bf16[2,4,120,128]{3,2,1,0:T(8,128)(2,1)} %shard_map.91) | data formatting | bytes 491520

commit v5 on v3

--- a/solution.py
+++ b/solution.py
@@ -175,7 +175,7 @@
             for a, b in ((next_t, r), (t, near_r), (t, far_r), (next_t, near_r), (next_t, far_r))
         )
         near_land, far_land = (6 - 5 * flip, 1 + 5 * flip)
-        far_in, far_in2 = (line(4), line(5))
+        far_in = line(4)
         inner = pl.ds(3, 2)
         return {
             "inner": halo(which, field, (0, 0), (own, inner), (past, inner), later),
@@ -193,10 +193,6 @@
             "from_far": halo(which, field, (4, 4 - flip), (own, line(3)), (own, far_in), far),
             "past_near": halo(which, field, (5, 5 + flip), (own, line(0)), (past, line(-1)), later),
             "on_far": halo(which, field, (7, 6 - flip), (own, far_in), (past, far_in), later),
-            "to_far2": halo(which, field, (8, 7), (own, line(2)), (own, 7 * flip), far),
-            "from_far2": halo(which, field, (8, 7), (own, line(2)), (own, far_in2), far),
-            "on_far2": halo(which, field, (9, 8), (own, far_in2), (past, far_in2), later),
-            "beyond": halo(which, field, (9, 8), (own, far_in), (past, far_in), later),
         }
 
     def when(flag, action):
@@ -366,7 +362,6 @@
     one["to_near"].start()
     when(has_next, one["diag_near"].start)
     when(has_next & fast, one["diag_far"].start)
-    when(slow, one["to_far2"].start)
     for name in ("inner", "first", "last"):
         when(has_next, one[name].start)
     loads[2].wait()
@@ -406,7 +401,7 @@
     when(has_prev & has_far, one["on_far"].wait_recv)
     for frame, total in enumerate(edge(act, first, 3)):
         to_mid(frame, 3, total)
-    when(fast, two["to_far"].start)
+    when(has_far, two["to_far"].start)
     when(has_next & fast, two["diag_far"].start)
     when(has_next, two["last"].start)
 
@@ -421,23 +416,14 @@
     to_hidden(0, edge(mid, second, 0))
     scatter_all()
 
-    @pl.when(slow)
-    def _():
-        one["from_far2"].wait_recv()
-        when(has_next, one["on_far2"].start)
-        when(has_prev, one["on_far2"].wait_recv)
-        for frame in range(2):
-            to_mid(frame, 4, product(act, first, frame, every, (4,), every))
-        when(has_next, two["beyond"].start)
-
     when(has_prev, two["last"].wait_recv)
     to_hidden(2, [product(mid, second, frame, every, (2,), every) for frame in range(2)])
     scatter_half(0)
     for frame in range(2):
         acc[frame, 3] = product(mid, second, frame, every, (3,), (0, 1))
-    when(fast, two["from_far"].wait_recv)
-    when(has_prev & fast, two["on_far"].wait_recv)
-    when(has_prev & slow, two["beyond"].wait_recv)
+    when(has_far, two["from_far"].wait_recv)
+    when(has_next & slow, two["on_far"].start)
+    when(has_prev & has_far, two["on_far"].wait_recv)
     to_hidden(3, edge(mid, second, 3))
     scatter_half(1)
 
@@ -454,11 +440,9 @@
         for name in ("inner", "first", "last", "diag_near"):
             when(has_next, copy[name].wait_send)
         when(has_next & fast, copy["diag_far"].wait_send)
-    when(has_far, one["to_far"].wait_send)
-    when(fast, two["to_far"].wait_send)
-    when(slow, one["to_far2"].wait_send)
-    for copy in (one["on_far"], one["on_far2"], two["beyond"]):
-        when(has_next & slow, copy.wait_send)
+    for copy in (one, two):
+        when(has_far, copy["to_far"].wait_send)
+        when(has_next & slow, copy["on_far"].wait_send)
 
     def gone(count, sem):
         sent = gathered.at[0, pl.ds(0, count)]
@@ -479,7 +463,7 @@
     square = (chans, chans)
     return pl.pallas_call(
         functools.partial(kernel, steps, blocks),
-        out_shape=jax.ShapeDtypeStruct(video.shape, video.dtype),
+        out_shape=pltpu.VMEM(video.shape, BF16),
         in_specs=[anywhere] * 9,
         out_specs=pl.BlockSpec(memory_space=pltpu.VMEM),
         scratch_shapes=[

time: 54 us -> 50.4 us (0.933)
  the two profiles are of different devices: /device:TPU:135 before, /device:TPU:353 now
where the time goes in v5:
time: 50.4 us; the launch traced here: 50.3 us
  Pallas kernels  49.6 us (98%)
  local copies, waits for them, and re-layouts  0.7 us (1%)
    pallas_call x1, Pallas kernels, local(): pl.pallas_call(functools.partial(kernel, steps, blocks), out_shape=pltpu....  49.6 us

profile of v5, /device:TPU:353, one launch (start us, length us, event | category | flops | bytes accessed | tf_op | source)
XLA Modules:
  0.0 50.3 jit_solution(6462617764127194546)
XLA Ops:
  0.0 49.6 %shard_map.91 = bf16[2,4,120,128]{3,2,1,0:T(8,128)(2,1)S(1)} custom-call(bf16[2,4,120,128]{3,2,1,0:T(8,128)(2,1)} %video_hbm.1, bf16[1,128]{1,0:T(2,128)(2,1)} %bitcast.2, bf16[3,3,3,128,128]{4,3,2,1,0:T(8,128)(2,1)} %first_hbm.1, bf16[3,3,3,128,128]{4,3,2,1,0:T(8,128)(2,1)} %second_hbm.1, bf16[1,128]{1,0:T(2,128)(2,1)} %bitcast.3, ...), custom_call_target="tpu_custom_call" | custom-call | tf_op jit(solution)/shard_map/pallas_call | solution.py:464
  49.6 0.7 %copy.11 = bf16[2,4,120,128]{3,2,1,0:T(8,128)(2,1)} copy(bf16[2,4,120,128]{3,2,1,0:T(8,128)(2,1)S(1)} %shard_map.91) | data formatting | bytes 491520

commit v6 on v5

--- a/solution.py
+++ b/solution.py
@@ -235,6 +235,8 @@
         hidden[q] = jnp.concatenate([one, two], axis=1).astype(BF16)
 
     parity = lax.rem(t, 2)
+    full = PER_ROW - 1
+    works = [lax.rem(t, PER_ROW) < full, t // 2 < full]
 
     def peer_copy(src, dst, send, recv, peer):
         return pltpu.make_async_remote_copy(
@@ -249,30 +251,33 @@
     def scatter_all():
         def body(j, _):
             peer = lax.rem(t + j, steps)
-            peer_copy(
+            copy = peer_copy(
                 hidden.at[peer // PER_ROW, lax.rem(peer, PER_ROW)],
                 gathered.at[0, t],
                 swap_send.at[0, 0],
                 swap_recv.at[0, 0],
                 peer,
-            ).start()
+            )
+            pl.when(lax.rem(peer, PER_ROW) < full)(copy.start)
             return 0
 
         lax.fori_loop(1, steps, body, 0)
-        pltpu.make_async_copy(
+        own_unit = pltpu.make_async_copy(
             hidden.at[t // PER_ROW, lax.rem(t, PER_ROW)], gathered.at[0, t], swap_recv.at[0, 0]
-        ).start()
+        )
+        pl.when(works[0])(own_unit.start)
 
     def scatter_half(odd):
         def send(j):
             spot = lax.rem(t // 2 + j, PER_ROW)
-            peer_copy(
+            copy = peer_copy(
                 hidden.at[2 + odd, spot],
                 gathered.at[1, t],
                 swap_send.at[0, 1 + odd],
                 swap_recv.at[0, 1],
                 2 * spot + odd,
-            ).start()
+            )
+            pl.when(spot < full)(copy.start)
 
         def body(j, _):
             send(j)
@@ -280,7 +285,7 @@
 
         lax.fori_loop(1, PER_ROW, body, 0)
         pl.when(parity != odd)(lambda: send(0))
-        pl.when(parity == odd)(
+        pl.when((parity == odd) & works[1])(
             pltpu.make_async_copy(
                 hidden.at[2 + odd, t // 2], gathered.at[1, t], swap_recv.at[0, 1]
             ).start
@@ -349,13 +354,13 @@
         pltpu.make_async_copy(answer.at[slot, t], home, arrived).start()
 
     def collect(index, rows):
-        block = returned.at[pl.ds(rows[0], len(rows))]
+        block = returned.at[pl.ds(rows[0], len(rows)), pl.ds(0, full)]
         pltpu.make_async_copy(block, block, swap_recv.at[1, index]).wait()
         for q in rows:
-            units = returned[q].astype(F32)
+            units = returned[q, 0:full].astype(F32)
             for frame in range(2):
-                cols = units[:, frame * UNIT : (frame + 1) * UNIT].reshape(COLS, chans)
-                result_ref[frame, place(q)] = cols[: COLS - UNIT].astype(BF16)
+                cols = units[:, frame * UNIT : (frame + 1) * UNIT].reshape(full * UNIT, chans)
+                result_ref[frame, place(q)] = cols.astype(BF16)
 
     one, two = (copies(0, act), copies(1, mid))
     when(has_far, one["to_far"].start)
@@ -429,8 +434,8 @@
 
     for load in loads[4:]:
         load.wait()
-    attend(0)
-    attend(1)
+    for slot in range(2):
+        pl.when(works[slot])(lambda slot=slot: attend(slot))
     collect(0, (0, 1))
     collect(1, (2,))
     collect(2, (3,))
@@ -448,12 +453,15 @@
         sent = gathered.at[0, pl.ds(0, count)]
         pltpu.make_async_copy(sent, sent, sem).wait()
 
-    gone(steps - 1, swap_send.at[0, 0])
-    for odd in range(2):
-        pl.when(parity == odd)(lambda odd=odd: gone(PER_ROW - 1, swap_send.at[0, 1 + odd]))
-        pl.when(parity != odd)(lambda odd=odd: gone(PER_ROW, swap_send.at[0, 1 + odd]))
+    for mine, count, sem in (
+        (works[0], steps - 2, swap_send.at[0, 0]),
+        (works[1] & (parity == 0), full, swap_send.at[0, 1]),
+        (works[1] & (parity == 1), full, swap_send.at[0, 2]),
+    ):
+        pl.when(mine)(lambda count=count, sem=sem: gone(count - 1, sem))
+        pl.when(~mine)(lambda count=count, sem=sem: gone(count, sem))
     for slot in range(2):
-        gone(steps - 1, swap_send.at[1, slot])
+        pl.when(works[slot])(lambda slot=slot: gone(steps - 1, swap_send.at[1, slot]))
 
 
 def local(video, norm_gain, first, second, attn_gain, query_w, key_w, value_w, out_w):

time: 50.4 us -> 50 us (level)
  no operation moved by 1% of the time
where the time goes in v6:
time: 50 us; the launch traced here: 49.9 us
  Pallas kernels  49.2 us (98%)
  local copies, waits for them, and re-layouts  0.7 us (1%)
    pallas_call x1, Pallas kernels, local(): pl.pallas_call(functools.partial(kernel, steps, blocks), out_shape=pltpu....  49.2 us

profile of v6, /device:TPU:353, one launch (start us, length us, event | category | flops | bytes accessed | tf_op | source)
XLA Modules:
  0.0 49.9 jit_solution(2391629935058583775)
XLA Ops:
  0.0 49.2 %shard_map.91 = bf16[2,4,120,128]{3,2,1,0:T(8,128)(2,1)S(1)} custom-call(bf16[2,4,120,128]{3,2,1,0:T(8,128)(2,1)} %video_hbm.1, bf16[1,128]{1,0:T(2,128)(2,1)} %bitcast.2, bf16[3,3,3,128,128]{4,3,2,1,0:T(8,128)(2,1)} %first_hbm.1, bf16[3,3,3,128,128]{4,3,2,1,0:T(8,128)(2,1)} %second_hbm.1, bf16[1,128]{1,0:T(2,128)(2,1)} %bitcast.3, ...), custom_call_target="tpu_custom_call" | custom-call | tf_op jit(solution)/shard_map/pallas_call | solution.py:472
  49.2 0.7 %copy.11 = bf16[2,4,120,128]{3,2,1,0:T(8,128)(2,1)} copy(bf16[2,4,120,128]{3,2,1,0:T(8,128)(2,1)S(1)} %shard_map.91) | data formatting | bytes 491520

commit v7 on v6

--- a/solution.py
+++ b/solution.py
@@ -69,6 +69,7 @@
     halo_recv,
     swap_send,
     swap_recv,
+    round_sem,
 ):
     t, r = (lax.axis_index("tm"), lax.axis_index("rows"))
     chans = video.shape[-1]
@@ -96,14 +97,22 @@
 
     barrier = pltpu.get_barrier_semaphore()
 
-    def greet(j, _):
-        peer = lax.rem(t + j, steps)
-        pl.semaphore_signal(barrier, inc=1, device_id={"tm": peer, "rows": r}, device_id_type=MESH)
-        return 0
-
-    lax.fori_loop(1, steps, greet, 0)
-
-    met = steps - 1
+    def partner(k):
+        return t + 2**k - 2 ** (k + 1) * lax.rem(t // 2**k, 2)
+
+    beside = t - 1 + 2 * lax.rem(t, 2)
+    has_beside = (beside >= 0) & (beside < steps)
+    rounds = steps.bit_length() - 1
+    for k in range(rounds):
+        pl.semaphore_signal(
+            barrier, inc=1, device_id={"tm": partner(k), "rows": r}, device_id_type=MESH
+        )
+    met = rounds + has_beside.astype(jnp.int32)
+
+    @pl.when(has_beside)
+    def _():
+        pl.semaphore_signal(barrier, inc=1, device_id={"tm": beside, "rows": r}, device_id_type=MESH)
+
     for side, there in ((1, has_above), (-1, has_below)):
         for shift, then in ((0, True), (1, has_next), (-1, has_prev)):
             present = there if shift == 0 else there & then
@@ -150,6 +159,14 @@
             act[frame + 2, row + 2] = padded(silu(rms_norm(wide, gain))).astype(BF16)
 
     pl.semaphore_wait(barrier, met)
+
+    def tell(k):
+        pl.semaphore_signal(
+            round_sem.at[k], inc=1, device_id={"tm": partner(k), "rows": r}, device_id_type=MESH
+        )
+
+    def told(k):
+        pl.semaphore_wait(round_sem.at[k], 1)
 
     def halo(which, field, slots, src, dst, device):
         return pltpu.make_async_remote_copy(
@@ -369,12 +386,15 @@
     when(has_next & fast, one["diag_far"].start)
     for name in ("inner", "first", "last"):
         when(has_next, one[name].start)
+    tell(0)
     loads[2].wait()
     for frame in range(2):
         for rows, span in groups:
             total = product(act, first, frame, range(2 - frame, 3), rows, span)
             for i, q in enumerate(rows):
                 acc[frame, q] = part(total, i)
+    told(0)
+    tell(1)
     for name in ("inner", "first", "last"):
         when(has_prev, one[name].wait_recv)
     for rows, span in groups:
@@ -394,6 +414,8 @@
             for frame in range(2)
         ]
 
+    told(1)
+    tell(2)
     one["from_near"].wait_recv()
     when(has_prev, one["past_near"].wait_recv)
     for frame, total in enumerate(edge(act, first, 0)):
@@ -401,6 +423,8 @@
     two["to_near"].start()
     when(has_next, two["diag_near"].start)
     when(has_next, two["first"].start)
+    told(2)
+    tell(3)
     when(has_far, one["from_far"].wait_recv)
     when(has_next & slow, one["on_far"].start)
     when(has_prev & has_far, one["on_far"].wait_recv)
@@ -410,6 +434,8 @@
     when(has_next & fast, two["diag_far"].start)
     when(has_next, two["last"].start)
 
+    told(3)
+    tell(4)
     loads[3].wait()
     for name in ("inner", "first"):
         when(has_prev, two[name].wait_recv)
@@ -419,6 +445,7 @@
     two["from_near"].wait_recv()
     when(has_prev, two["past_near"].wait_recv)
     to_hidden(0, edge(mid, second, 0))
+    told(4)
     scatter_all()
 
     when(has_prev, two["last"].wait_recv)
@@ -496,6 +523,7 @@
             pltpu.SemaphoreType.DMA((2, 10)),
             pltpu.SemaphoreType.DMA((2, 3)),
             pltpu.SemaphoreType.DMA((2, 3)),
+            pltpu.SemaphoreType.REGULAR((5,)),
         ],
         compiler_params=pltpu.CompilerParams(
             collective_id=0, has_side_effects=True, vmem_limit_bytes=56 * 1024 * 1024

time: 50 us -> 49.7 us (level)
  the two profiles are of different devices: /device:TPU:353 before, /device:TPU:7 now
where the time goes in v7:
time: 49.7 us; the launch traced here: 49.6 us
  Pallas kernels  48.9 us (98%)
  local copies, waits for them, and re-layouts  0.7 us (1%)
    pallas_call x1, Pallas kernels, local(): pl.pallas_call(functools.partial(kernel, steps, blocks), out_shape=pltpu....  48.9 us

profile of v7, /device:TPU:7, one launch (start us, length us, event | category | flops | bytes accessed | tf_op | source)
XLA Modules:
  0.0 49.6 jit_solution(5115915958664963473)
XLA Ops:
  0.0 48.9 %shard_map.91 = bf16[2,4,120,128]{3,2,1,0:T(8,128)(2,1)S(1)} custom-call(bf16[2,4,120,128]{3,2,1,0:T(8,128)(2,1)} %video_hbm.1, bf16[1,128]{1,0:T(2,128)(2,1)} %bitcast.2, bf16[3,3,3,128,128]{4,3,2,1,0:T(8,128)(2,1)} %first_hbm.1, bf16[3,3,3,128,128]{4,3,2,1,0:T(8,128)(2,1)} %second_hbm.1, bf16[1,128]{1,0:T(2,128)(2,1)} %bitcast.3, ...), custom_call_target="tpu_custom_call" | custom-call | tf_op jit(solution)/shard_map/pallas_call | solution.py:499
  48.9 0.7 %copy.11 = bf16[2,4,120,128]{3,2,1,0:T(8,128)(2,1)} copy(bf16[2,4,120,128]{3,2,1,0:T(8,128)(2,1)S(1)} %shard_map.91) | data formatting | bytes 491520
